TPU v7x, 32 devices: a whole 2x2x4 slice. The times are simulated.
32 devices in a mesh: shard: 8 (over z, y), rep: 4 (over x, core).
Axes of the slice: x: 2, y: 2, z: 4, core: 2. Of those that a mesh axis runs over, the one named last changes fastest.
Arguments:
- tokens: bfloat16 [4096, 768], P(('shard', 'rep')), may hold values from -6 to 6
- labels: int32 [4096], P(('shard', 'rep')), may hold values from 0 to 3, as said below
- w_qkv: bfloat16 [768, 2304], P('shard'), may hold values from -0.21875 to 0.21875
- bias_qv: bfloat16 [1536], P('shard'), may hold values from -3 to 3
- w_out: bfloat16 [768, 768], P('shard'), may hold values from -0.875 to 0.875
- bias_out: bfloat16 [768], P('shard'), may hold values from -3 to 3
- w_in: bfloat16 [768, 3072], P('shard'), may hold values from -0.21875 to 0.21875
- bias_in: bfloat16 [3072], P('shard'), may hold values from -3 to 3
- w_back: bfloat16 [3072, 768], P('shard'), may hold values from -0.109375 to 0.109375
- bias_back: bfloat16 [768], P('shard'), may hold values from -3 to 3
- gain_one: bfloat16 [768], P('shard'), may hold values from 0.099609375 to 1.8984375
- shift_one: bfloat16 [768], P('shard'), may hold values from -3 to 3
- gain_two: bfloat16 [768], P('shard'), may hold values from 0.099609375 to 1.8984375
- shift_two: bfloat16 [768], P('shard'), may hold values from -3 to 3
- cotangent: bfloat16 [4096, 768], P(('shard', 'rep')), may hold values from -6 to 6
Outputs:
- output: bfloat16 [4096, 768], P(('shard', 'rep'))
- grad_tokens: float32 [4096, 768], P(('shard', 'rep'))
- grad_w_qkv: float32 [768, 2304], P('shard')
- grad_bias_qv: float32 [1536], P('shard')
- grad_w_out: float32 [768, 768], P('shard')
- grad_bias_out: float32 [768], P('shard')
- grad_w_in: float32 [768, 3072], P('shard')
- grad_bias_in: float32 [3072], P('shard')
- grad_w_back: float32 [3072, 768], P('shard')
- grad_bias_back: float32 [768], P('shard')
- grad_gain_one: float32 [768], P('shard')
- grad_shift_one: float32 [768], P('shard')
- grad_gain_two: float32 [768], P('shard')
- grad_shift_two: float32 [768], P('shard')
Inputs may be any that keep to these rules, and one draw needn't show every extreme that they name: `labels`: within each block of 128 slots of one device, live tokens come first and number at least 85; each positive label marks one sequence, a contiguous run, at most 3 on a device; one device holds a single sequence of all 128 slots.
All inputs are finite; a program needn't handle non-finite values.
Results may differ from a plain program's by a relative error of at most 0.012.
The roundings to bfloat16 on the way count: a program that leaves them out, or rounds other values in their place, can miss the bound.
Values may be sent and summed in bfloat16 or wider, within the bound.
A program may use at most 128 MiB of HBM per device.

v0:
```python
import math

import jax
import jax.numpy as jnp
from jax import lax
from jax.sharding import PartitionSpec as P

HEADS = 12
HEAD_DIM = 64


EPSILON = 1e-05


def normalize(summed, gain_row, shift_row):
    average = jnp.mean(summed, -1, keepdims=True)
    centred = summed - average
    inv_scale = lax.rsqrt(jnp.mean(centred * centred, -1, keepdims=True) + EPSILON)
    unit_rows = centred * inv_scale
    return (
        unit_rows * gain_row.astype(jnp.float32) + shift_row.astype(jnp.float32),
        unit_rows,
        inv_scale,
    )


def norm_back(grad_unit, unit_rows, inv_scale):
    centred_grad = grad_unit - jnp.mean(grad_unit, -1, keepdims=True)
    return inv_scale * (
        centred_grad - unit_rows * jnp.mean(grad_unit * unit_rows, -1, keepdims=True)
    )


def gelu_exact(inputs):
    return jax.nn.gelu(inputs, approximate=False)


def body(
    tokens,
    labels,
    w_qkv,
    bias_qv,
    w_out,
    bias_out,
    w_in,
    bias_in,
    w_back,
    bias_back,
    gain_one,
    shift_one,
    gain_two,
    shift_two,
    cotangent,
):
    gathered = (
        lax.all_gather(w_qkv, "shard", axis=0, tiled=True),
        lax.all_gather(bias_qv, "shard", axis=0, tiled=True),
        lax.all_gather(w_out, "shard", axis=0, tiled=True),
        lax.all_gather(bias_out, "shard", axis=0, tiled=True),
        lax.all_gather(w_in, "shard", axis=0, tiled=True),
        lax.all_gather(bias_in, "shard", axis=0, tiled=True),
        lax.all_gather(w_back, "shard", axis=0, tiled=True),
        lax.all_gather(bias_back, "shard", axis=0, tiled=True),
        lax.all_gather(gain_one, "shard", axis=0, tiled=True),
        lax.all_gather(shift_one, "shard", axis=0, tiled=True),
        lax.all_gather(gain_two, "shard", axis=0, tiled=True),
        lax.all_gather(shift_two, "shard", axis=0, tiled=True),
    )
    (
        full_qkv,
        full_bias_qv,
        full_out,
        full_bias_out,
        full_in,
        full_bias_in,
        full_back,
        full_bias_back,
        full_gain_one,
        full_shift_one,
        full_gain_two,
        full_shift_two,
    ) = gathered
    model_width = full_out.shape[0]
    row_count = tokens.shape[0]
    score_scale = 1.0 / math.sqrt(HEAD_DIM)
    qkv = jnp.dot(tokens, full_qkv, preferred_element_type=jnp.float32)
    bias_float = full_bias_qv.astype(jnp.float32)
    query_rows = (qkv[:, :model_width] + bias_float[:model_width]).astype(jnp.bfloat16)
    key_rows = qkv[:, model_width : 2 * model_width].astype(jnp.bfloat16)
    value_rows = (qkv[:, 2 * model_width :] + bias_float[model_width:]).astype(jnp.bfloat16)
    query_heads = query_rows.reshape(row_count, HEADS, HEAD_DIM)
    key_heads = key_rows.reshape(row_count, HEADS, HEAD_DIM)
    value_heads = value_rows.reshape(row_count, HEADS, HEAD_DIM)
    scores = (
        jnp.einsum("qhd,khd->hqk", query_heads, key_heads, preferred_element_type=jnp.float32)
        * score_scale
    )
    same_doc = labels[:, None] == labels[None, :]
    scores = jnp.where(same_doc[None], scores, -1000000000.0)
    highest = jnp.max(scores, -1, keepdims=True)
    exponent = jnp.exp(scores - highest)
    attention = exponent / jnp.sum(exponent, -1, keepdims=True)
    attention_low = attention.astype(jnp.bfloat16)
    mixed_heads = jnp.einsum(
        "hqk,khd->qhd", attention_low, value_heads, preferred_element_type=jnp.float32
    )
    mixed_heads = mixed_heads.reshape(row_count, model_width).astype(jnp.bfloat16)
    attn_out = jnp.dot(
        mixed_heads, full_out, preferred_element_type=jnp.float32
    ) + full_bias_out.astype(jnp.float32)
    first_out, unit_one, scale_one = normalize(
        tokens.astype(jnp.float32) + attn_out, full_gain_one, full_shift_one
    )
    first_low = first_out.astype(jnp.bfloat16)
    inner_sum = jnp.dot(
        first_low, full_in, preferred_element_type=jnp.float32
    ) + full_bias_in.astype(jnp.float32)
    activated = gelu_exact(inner_sum).astype(jnp.bfloat16)
    branch = jnp.dot(
        activated, full_back, preferred_element_type=jnp.float32
    ) + full_bias_back.astype(jnp.float32)
    final_out, unit_two, scale_two = normalize(first_out + branch, full_gain_two, full_shift_two)
    live_rows = (labels > 0).astype(jnp.float32)[:, None]
    output = (final_out * live_rows).astype(jnp.bfloat16)
    (
        back_qkv,
        unused_bias_qv,
        back_out,
        unused_bias_out,
        back_in,
        unused_bias_in,
        back_weights,
        unused_bias_back,
        back_gain_one,
        unused_shift_one,
        back_gain_two,
        unused_shift_two,
    ) = gathered
    grad_final = cotangent.astype(jnp.float32) * live_rows
    d_gain_two = jnp.sum(grad_final * unit_two, 0)
    d_shift_two = jnp.sum(grad_final, 0)
    grad_mid = norm_back(grad_final * back_gain_two.astype(jnp.float32), unit_two, scale_two)
    grad_branch = grad_mid.astype(jnp.bfloat16)
    d_w_back = jnp.einsum("tf,td->fd", activated, grad_branch, preferred_element_type=jnp.float32)
    d_bias_back = jnp.sum(grad_branch.astype(jnp.float32), 0)
    grad_act = jnp.einsum(
        "td,fd->tf", grad_branch, back_weights, preferred_element_type=jnp.float32
    )
    unused_value, gelu_pull = jax.vjp(gelu_exact, inner_sum)
    grad_inner = gelu_pull(grad_act)[0].astype(jnp.bfloat16)
    d_w_in = jnp.einsum("td,tf->df", first_low, grad_inner, preferred_element_type=jnp.float32)
    d_bias_in = jnp.sum(grad_inner.astype(jnp.float32), 0)
    grad_first = (
        jnp.einsum("tf,df->td", grad_inner, back_in, preferred_element_type=jnp.float32) + grad_mid
    )
    d_gain_one = jnp.sum(grad_first * unit_one, 0)
    d_shift_one = jnp.sum(grad_first, 0)
    grad_res = norm_back(grad_first * back_gain_one.astype(jnp.float32), unit_one, scale_one)
    grad_attn = grad_res.astype(jnp.bfloat16)
    d_w_out = jnp.einsum("td,te->de", mixed_heads, grad_attn, preferred_element_type=jnp.float32)
    d_bias_out = jnp.sum(grad_attn.astype(jnp.float32), 0)
    grad_mixed = jnp.einsum(
        "te,de->td", grad_attn, back_out, preferred_element_type=jnp.float32
    ).astype(jnp.bfloat16)
    grad_mixed_heads = grad_mixed.reshape(row_count, HEADS, HEAD_DIM)
    grad_attention = jnp.einsum(
        "qhd,khd->hqk", grad_mixed_heads, value_heads, preferred_element_type=jnp.float32
    )
    row_dot = jnp.sum(attention * grad_attention, -1, keepdims=True)
    grad_scores = (attention * (grad_attention - row_dot)).astype(jnp.bfloat16)
    grad_query = (
        jnp.einsum("hqk,khd->qhd", grad_scores, key_heads, preferred_element_type=jnp.float32)
        * score_scale
    ).astype(jnp.bfloat16)
    grad_keys = (
        jnp.einsum("hqk,qhd->khd", grad_scores, query_heads, preferred_element_type=jnp.float32)
        * score_scale
    ).astype(jnp.bfloat16)
    grad_values = jnp.einsum(
        "hqk,qhd->khd", attention_low, grad_mixed_heads, preferred_element_type=jnp.float32
    ).astype(jnp.bfloat16)
    grad_query = grad_query.reshape(row_count, model_width)
    grad_keys = grad_keys.reshape(row_count, model_width)
    grad_values = grad_values.reshape(row_count, model_width)
    grad_qkv = jnp.concatenate([grad_query, grad_keys, grad_values], 1)
    d_w_qkv = jnp.einsum("td,te->de", tokens, grad_qkv, preferred_element_type=jnp.float32)
    d_bias_qv = jnp.concatenate(
        [jnp.sum(grad_query.astype(jnp.float32), 0), jnp.sum(grad_values.astype(jnp.float32), 0)], 0
    )
    grad_tokens = (
        jnp.einsum("te,de->td", grad_qkv, back_qkv, preferred_element_type=jnp.float32) + grad_res
    )
    owned = (
        lax.psum_scatter(d_w_qkv, "shard", scatter_dimension=0, tiled=True),
        lax.psum_scatter(d_bias_qv, "shard", scatter_dimension=0, tiled=True),
        lax.psum_scatter(d_w_out, "shard", scatter_dimension=0, tiled=True),
        lax.psum_scatter(d_bias_out, "shard", scatter_dimension=0, tiled=True),
        lax.psum_scatter(d_w_in, "shard", scatter_dimension=0, tiled=True),
        lax.psum_scatter(d_bias_in, "shard", scatter_dimension=0, tiled=True),
        lax.psum_scatter(d_w_back, "shard", scatter_dimension=0, tiled=True),
        lax.psum_scatter(d_bias_back, "shard", scatter_dimension=0, tiled=True),
        lax.psum_scatter(d_gain_one, "shard", scatter_dimension=0, tiled=True),
        lax.psum_scatter(d_shift_one, "shard", scatter_dimension=0, tiled=True),
        lax.psum_scatter(d_gain_two, "shard", scatter_dimension=0, tiled=True),
        lax.psum_scatter(d_shift_two, "shard", scatter_dimension=0, tiled=True),
    )
    summed = lax.psum(
        (
            owned[0],
            owned[1],
            owned[2],
            owned[3],
            owned[4],
            owned[5],
            owned[6],
            owned[7],
            owned[8],
            owned[9],
            owned[10],
            owned[11],
        ),
        "rep",
    )
    return (
        output,
        grad_tokens,
        summed[0],
        summed[1],
        summed[2],
        summed[3],
        summed[4],
        summed[5],
        summed[6],
        summed[7],
        summed[8],
        summed[9],
        summed[10],
        summed[11],
    )


def solution(mesh):
    placed = (
        P(("shard", "rep"), None),
        P(("shard", "rep")),
        P("shard", None),
        P("shard"),
        P("shard", None),
        P("shard"),
        P("shard", None),
        P("shard"),
        P("shard", None),
        P("shard"),
        P("shard"),
        P("shard"),
        P("shard"),
        P("shard"),
        P(("shard", "rep"), None),
    )
    return jax.shard_map(
        body,
        mesh=mesh,
        in_specs=placed,
        out_specs=(
            P(("shard", "rep"), None),
            P(("shard", "rep"), None),
            P("shard", None),
            P("shard"),
            P("shard", None),
            P("shard"),
            P("shard", None),
            P("shard"),
            P("shard", None),
            P("shard"),
            P("shard"),
            P("shard"),
            P("shard"),
            P("shard"),
        ),
        check_vma=False,
    )
```

profile of v0, /device:TPU:0, one launch (start us, length us, event | category | flops | bytes accessed | tf_op | source)
XLA Modules:
  0.0 940.5 jit_solution(13518387769844771062)
XLA Ops:
  13.7 39.5 %all-reduce.18 = (bf16[1536]{0:T(1024)(128)(2,1)S(1)}, bf16[768]{0:T(1024)(128)(2,1)S(1)}, bf16[768]{0:T(1024)(128)(2,1)S(1)}, bf16[768]{0:T(1024)(128)(2,1)S(1)...) all-reduce(bf16[1536]{0:T(1024)(128)(2,1)S(1)} %dynamic-update-slic, ...), channel_id=1, replica_groups=mesh['shard'=8,'rep'=4] {'shard'}, use_global_device_ids=true, to_apply=%add | all-reduce | flops 6144 | bytes 24576
  53.2 26.1 %all-gather = bf16[8,1,384]{2,1,0:T(2,128)(2,1)S(1)} all-gather(bf16[1,1,384]{2,1,0:T(2,128)(2,1)S(1)} %reshape.161), channel_id=1, replica_groups=mesh['shard'=8,'rep'=4] {'shard'}, dimensions={0}, use_global_device_ids=true | all-gather | bytes 6912 | tf_op jit(solution)/shard_map/all_gather | solution.py:61
  79.6 2.6 fusion.45
  84.8 36.0 %all-gather.8.cloned.1.call-done = bf16[768,768]{1,0:T(8,128)(2,1)} async-done(((bf16[96,768]{1,0:T(8,128)(2,1)}), bf16[768,768]{1,0:T(8,128)(2,1)}) %all-gather.8.cloned.1.call-update) | async-done | bytes 1179664 | tf_op jit(solution)/shard_map/all_gather | solution.py:58
  122.7 78.9 %all-gather.10.cloned.1.call-done = bf16[768,3072]{1,0:T(8,128)(2,1)} async-done(((bf16[96,3072]{1,0:T(8,128)(2,1)}), bf16[768,3072]{1,0:T(8,128)(2,1)}) %all-gather.10.cloned.1.call-update) | async-done | bytes 4718608 | tf_op jit(solution)/shard_map/all_gather | solution.py:60
  201.7 8.4 multiply_convert_fusion
  210.0 71.7 %all-gather.12.cloned.1.call-done = bf16[3072,768]{1,0:T(8,128)(2,1)} async-done(((bf16[384,768]{1,0:T(8,128)(2,1)}), bf16[3072,768]{1,0:T(8,128)(2,1)}) %all-gather.12.cloned.1.call-update) | async-done | bytes 4718608 | tf_op jit(solution)/shard_map/all_gather | solution.py:62
  281.8 3.4 fusion.44
  287.7 2.5 convert_reduce_fusion
  290.2 2.4 multiply_reduce_fusion.2
  301.7 4.0 convolution_bitcast_fusion
  305.7 8.0 copy.64
  316.3 5.3 fusion.36
  321.8 5.1 fusion.27
  327.0 114.0 %reduce-scatter.13.cloned.1.call-done = f32[96,2304]{1,0:T(8,128)} async-done(((f32[768,2304]{1,0:T(8,128)}), f32[96,2304]{1,0:T(8,128)}) %reduce-scatter.13.cloned.1.call-update) | async-done | bytes 884752
  441.0 2.6 copy.65
  443.5 69.3 %reduce-scatter.7.cloned.1.call-done = f32[96,768]{1,0:T(8,128)} async-done(((f32[768,768]{1,0:T(8,128)}), f32[96,768]{1,0:T(8,128)}) %reduce-scatter.7.cloned.1.call-update) | async-done | bytes 294928 | tf_op jit(solution)/shard_map/reduce_scatter | solution.py:196
  512.8 166.4 %reduce-scatter.9.cloned.1.call-done = f32[96,3072]{1,0:T(8,128)} async-done(((f32[768,3072]{1,0:T(8,128)}), f32[96,3072]{1,0:T(8,128)}) %reduce-scatter.9.cloned.1.call-update) | async-done | bytes 1179664 | tf_op jit(solution)/shard_map/reduce_scatter | solution.py:198
  679.2 166.4 %reduce-scatter.11.cloned.1.call-done = f32[384,768]{1,0:T(8,128)} async-done(((f32[3072,768]{1,0:T(8,128)}), f32[384,768]{1,0:T(8,128)}) %reduce-scatter.11.cloned.1.call-update) | async-done | bytes 1179664 | tf_op jit(solution)/shard_map/reduce_scatter | solution.py:200
  849.3 36.7 %all-reduce.15 = (f32[1536]{0:T(1024)}, f32[768]{0:T(1024)}, f32[3072]{0:T(1024)}, f32[768]{0:T(1024)}, f32[768]{0:T(1024)}, /*index=5*/f32[768]{0:T(1024)}, f32[768]{0:T(1024)}, f32[768]{0:T(1024)S(1)}) all-reduce(f32[1536]{0:T(1024)S(1)} %pad_maximum_fusion.3, ...), channel_id=3, replica_groups=mesh['shard'=8,'rep'=4] {'shard'}, use_global_device_ids=true, to_apply=%region_15.16.clone | all-reduce | flops 9216 | bytes 73728
  893.5 7.0 all-reduce.16
  900.5 3.3 convolution_add_fusion.2
  903.8 24.7 %all-reduce.21.cloned.1.call-done = (f32[96,2304]{0,1:T(8,128)}, f32[96,768]{1,0:T(8,128)}, f32[96,3072]{1,0:T(8,128)}, f32[384,768]{1,0:T(8,128)}) async-done(((f32[96,2304]{0,1:T(8,128)}, f32[96,768]{1,0:T(8,128)}, f32[96,3072]{1,0:T(8,128)}, f32[384,768]{1,0:T(8,128)}), (f32[96,2304]{0,1:T(8,128)}, f32[96,768]{1,0:T(8,128)}, f32[96,3072]{1,0:T(8,128)}, ...) | async-done | bytes 3538960 | tf_op jit(solution)/shard_map/psum | solution.py:207
  928.6 2.7 copy.59
  (167 shorter events, 35.7 us)
Async XLA Ops:
  7.2 5.3 copy-start.28
  7.2 5.5 copy-start.29
  7.2 5.8 copy-start.30
  7.2 6.0 copy-start.31
  7.3 6.2 copy-start.32
  7.3 45.9 %copy-start.25 = (bf16[384]{0:T(512)(128)(2,1)S(1)}, bf16[384]{0:T(512)(128)(2,1)}, u32[]{:S(2)}) copy-start(bf16[384]{0:T(512)(128)(2,1)} %param.22) | copy-start | bytes 2308
  7.3 72.1 %copy-start.23 = (s32[128]{0:T(128)S(1)}, s32[128]{0:T(128)}, u32[]{:S(2)}) copy-start(s32[128]{0:T(128)} %param.16) | copy-start | bytes 1540
  7.3 72.3 %copy-start.3 = (bf16[128,768]{1,0:T(8,128)(2,1)S(1)}, bf16[128,768]{1,0:T(8,128)(2,1)}, u32[]{:S(2)}) copy-start(bf16[128,768]{1,0:T(8,128)(2,1)} %param.15) | copy-start | bytes 589828
  7.3 72.2 %all-gather.6.cloned.1.call-start = ((), (), s32[]{:S(2)}) async-start(), calls=%async_computation.4 | async-start | bytes 3981312 | tf_op jit(solution)/shard_map/all_gather | solution.py:56
  8.0 112.8 %all-gather.8.cloned.1.call-start = ((), (), s32[]{:S(2)}) async-start(), calls=%async_computation.5 | async-start | bytes 1327104 | tf_op jit(solution)/shard_map/all_gather | solution.py:58
  8.8 192.9 %all-gather.10.cloned.1.call-start = ((), (), s32[]{:S(2)}) async-start(), calls=%async_computation.6 | async-start | bytes 5308416 | tf_op jit(solution)/shard_map/all_gather | solution.py:60
  9.5 272.2 %all-gather.12.cloned.1.call-start = ((), (), s32[]{:S(2)}) async-start(), calls=%async_computation.7 | async-start | bytes 5308416 | tf_op jit(solution)/shard_map/all_gather | solution.py:62
  10.1 430.9 %reduce-scatter.13.cloned.1.call-start = ((), (), s32[]{:S(2)}) async-start(), calls=%async_computation.11 | async-start | bytes 7962624
  122.5 170.1 %copy-start.15 = (f32[128]{0:T(128)}, f32[128]{0:T(128)S(1)}, u32[]{:S(2)}) copy-start(f32[128]{0:T(128)S(1)} %broadcast_multiply_fusion.5) | copy-start | bytes 1540
  122.7 169.9 %copy-start.18 = (f32[128]{0:T(128)}, f32[128]{0:T(128)S(1)}, u32[]{:S(2)}) copy-start(f32[128]{0:T(128)S(1)} %add_rsqrt_fusion.1) | copy-start | bytes 1540
  281.8 5.9 slice-start
  281.8 5.9 slice-start.1
  281.8 5.9 copy-start.34
  293.4 20.4 %copy-start.1 = (f32[128,768]{1,0:T(8,128)}, f32[128,768]{1,0:T(8,128)S(1)}, u32[]{:S(2)}) copy-start(f32[128,768]{1,0:T(8,128)S(1)} %get-tuple-element.94) | copy-start | bytes 1179652
  313.7 199.1 %reduce-scatter.7.cloned.1.call-start = ((), (), s32[]{:S(2)}) async-start(), calls=%async_computation.8 | async-start | bytes 2654208 | tf_op jit(solution)/shard_map/reduce_scatter | solution.py:196
  315.6 363.5 %reduce-scatter.9.cloned.1.call-start = ((), (), s32[]{:S(2)}) async-start(), calls=%async_computation.9 | async-start | bytes 10616832 | tf_op jit(solution)/shard_map/reduce_scatter | solution.py:198
  321.6 524.0 %reduce-scatter.11.cloned.1.call-start = ((), (), s32[]{:S(2)}) async-start(), calls=%async_computation.10 | async-start | bytes 10616832 | tf_op jit(solution)/shard_map/reduce_scatter | solution.py:200
  326.9 601.6 %all-reduce.21.cloned.1.call-start = ((), (), s32[]{:S(2)}) async-start(), calls=%async_computation.12 | async-start | bytes 7667712 | tf_op jit(solution)/shard_map/psum | solution.py:207
  845.6 54.9 %copy-start = (bf16[768,2304]{1,0:T(8,128)(2,1)S(1)}, bf16[768,2304]{1,0:T(8,128)(2,1)}, u32[]{:S(2)}) copy-start(bf16[768,2304]{1,0:T(8,128)(2,1)} %all-gather.6.cloned.1.call-done) | copy-start | bytes 10616836
  (24 other events, 57.6 us)
Sparse Core Ops, SparseCore 0:
  10.3 68.5 all-gather.5
  81.1 39.6 all-gather.7
  123.0 78.6 all-gather.9
  203.7 78.0 all-gather.11
  313.8 127.1 reduce-scatter.12
  444.7 68.0 reduce-scatter.6
  516.8 162.2 reduce-scatter.8
  683.2 162.3 reduce-scatter.10
  849.0 79.5 all-reduce.20
where the time goes:
time: 941 us
  waiting for transfers between devices  730 us (78%)
  blocking collectives  109 us (12%)
  matrix products  47.7 us (5%)
  local copies, waits for them, and re-layouts  30.3 us (3%)
  between operations  17.9 us (2%)
    reduce_scatter x1, waiting for transfers between devices, body(): lax.psum_scatter(d_w_back, 'shard', scatter_dimension=0, tiled=True)  166 us
    reduce_scatter x1, waiting for transfers between devices, body(): lax.psum_scatter(d_w_in, 'shard', scatter_dimension=0, tiled=True)  166 us
    unnamed x10, waiting for transfers between devices  117 us
    all_gather x1, waiting for transfers between devices, body(): lax.all_gather(w_in, 'shard', axis=0, tiled=True)  78.9 us
    unnamed x2, blocking collectives  76.2 us
    all_gather x1, waiting for transfers between devices, body(): lax.all_gather(w_back, 'shard', axis=0, tiled=True)  71.7 us
    reduce_scatter x1, waiting for transfers between devices, body(): lax.psum_scatter(d_w_out, 'shard', scatter_dimension=0, tiled=True)  69.3 us
    all_gather x1, waiting for transfers between devices, body(): lax.all_gather(w_out, 'shard', axis=0, tiled=True)  36 us
  transfers between devices with their start and end apart: 9, of which 8 were waited for; matrix products, arithmetic and copies ran while one was open for 5% of the time, Pallas kernels for 0%

commit v1 on v0

--- a/solution.py
+++ b/solution.py
@@ -1,15 +1,497 @@
+import functools
 import math
 
 import jax
 import jax.numpy as jnp
 from jax import lax
+from jax.experimental import pallas as pl
+from jax.experimental.pallas import tpu as pltpu
 from jax.sharding import PartitionSpec as P
 
 HEADS = 12
 HEAD_DIM = 64
-
-
 EPSILON = 1e-05
+MESH = pl.DeviceIdType.MESH
+QUAD = 4
+
+
+class Place:
+    def __init__(self, n_shard):
+        self.n = n_shard
+        self.half = n_shard // 2
+        self.s = lax.axis_index("shard")
+        self.r = lax.axis_index("rep")
+        self.base = self.r - self.r % QUAD
+        self.x = (self.r % QUAD) // 2
+        self.c = self.r % 2
+        z, y = self.s // 2, self.s % 2
+        self.p = z * (1 - y) + (n_shard - 1 - z) * y
+        self.core_peer = (self.s, self.base + self.x * 2 + (1 - self.c))
+        self.chip_peer = (self.s, self.base + (1 - self.x) * 2 + self.c)
+        self.right = (self.at(1), self.r)
+        self.left = (self.at(-1), self.r)
+
+    def at(self, offset):
+        p = (self.p + offset + 2 * self.n) % self.n
+        upper = p // self.half
+        return (1 - upper) * 2 * p + upper * (2 * (self.n - 1 - p) + 1)
+
+    def greet(self):
+        barrier = pltpu.get_barrier_semaphore()
+        targets = [((self.s + k) % self.n, self.r) for k in range(1, self.n)]
+        targets += [self.core_peer, self.chip_peer]
+        for device in targets:
+            pl.semaphore_signal(barrier, inc=1, device_id=device, device_id_type=MESH)
+        pl.semaphore_wait(barrier, len(targets))
+
+
+def remote(src, dst, send, recv, device):
+    return pltpu.make_async_remote_copy(
+        src_ref=src,
+        dst_ref=dst,
+        send_sem=send,
+        recv_sem=recv,
+        device_id=device,
+        device_id_type=MESH,
+    )
+
+
+def cols(index, width):
+    return pl.ds(pl.multiple_of(index * width, 128), width)
+
+
+def hops(n, unit):
+    more, less = n // 2, n - 1 - n // 2
+    return (more, less) if unit == 0 else (less, more)
+
+
+def gather_kernel(n, *refs):
+    ins, outs = refs[:5], refs[5:10]
+    own_sem, ring_s, ring_r, chip_s, chip_r, core_s, core_r, far_s, far_r, small_s, small_r = refs[10:]
+    me = Place(n)
+    widths = (outs[0].shape[2] // 2, outs[1].shape[2] // 2, outs[2].shape[2] // 4)
+
+    def part(k, block, x):
+        if k < 2:
+            return outs[k].at[block, :, cols(me.c, widths[k])]
+        if k == 2:
+            return outs[2].at[block, :, cols(me.c * 2 + x, widths[2])]
+        return outs[3].at[block, me.c * 2 + x]
+
+    def mine(k):
+        if k < 2:
+            return ins[k].at[:, cols(me.c, widths[k])]
+        if k == 2:
+            return ins[2].at[:, cols(me.c * 2 + me.x, widths[2])]
+        return ins[3].at[me.c * 2 + me.x]
+
+    me.greet()
+    pending = []
+
+    def ring(k, way, t):
+        block = me.at(-t if way == 0 else t)
+        src = mine(k) if t == 0 else part(k, block, me.x)
+        copy = remote(
+            src,
+            part(k, block, me.x),
+            ring_s.at[k, way, t],
+            ring_r.at[k, way, t],
+            me.right if way == 0 else me.left,
+        )
+        copy.start()
+        pending.append(copy)
+
+    def from_ring(k, way, t):
+        block = me.at(-1 - t if way == 0 else 1 + t)
+        here = part(k, block, me.x)
+        remote(here, here, ring_s.at[k, way, t], ring_r.at[k, way, t], me.left).wait_recv()
+        return block
+
+    def to_peer(k, block, x, send, recv, device):
+        copy = remote(part(k, block, x), part(k, block, x), send, recv, device)
+        copy.start()
+        pending.append(copy)
+
+    order = (2, 3, 0, 1)
+    for k in order:
+        for way in range(2):
+            ring(k, way, 0)
+    for j in range(1, n):
+        other = (me.s + j) % n
+        copy = remote(ins[4], outs[4].at[me.s], small_s.at[j], small_r.at[j], (other, me.r))
+        copy.start()
+        pending.append(copy)
+    own = [
+        pltpu.make_async_copy(ins[k], outs[k].at[me.s], own_sem.at[k]) for k in range(5)
+    ]
+    for copy in own:
+        copy.start()
+
+    def from_chip(k, way, t):
+        block = me.at(-1 - t if way == 0 else 1 + t)
+        here = part(k, block, 1 - me.x)
+        i = k - 2
+        remote(here, here, chip_s.at[i, way, t], chip_r.at[i, way, t], me.chip_peer).wait_recv()
+        to_peer(k, block, 1 - me.x, far_s.at[i, way, t], far_r.at[i, way, t], me.core_peer)
+
+    most = n // 2
+    for t in range(most + 1):
+        for k in order:
+            unit = 1 if k > 1 else 0
+            for way in range(2):
+                last = hops(n, unit)[way]
+                if t < last:
+                    block = from_ring(k, way, t)
+                    if t + 1 < last:
+                        ring(k, way, t + 1)
+                    if unit:
+                        to_peer(
+                            k,
+                            block,
+                            me.x,
+                            chip_s.at[k - 2, way, t],
+                            chip_r.at[k - 2, way, t],
+                            me.chip_peer,
+                        )
+                    to_peer(
+                        k, block, me.x, core_s.at[k, way, t], core_r.at[k, way, t], me.core_peer
+                    )
+        for k in (2, 3):
+            for way in range(2):
+                if 0 <= t - 1 < hops(n, 1)[way]:
+                    from_chip(k, way, t - 1)
+
+    def peer_part(k, block, x):
+        if k < 2:
+            return outs[k].at[block, :, cols(1 - me.c, widths[k])]
+        if k == 2:
+            return outs[2].at[block, :, cols((1 - me.c) * 2 + x, widths[2])]
+        return outs[3].at[block, (1 - me.c) * 2 + x]
+
+    for k in range(4):
+        unit = 1 if k > 1 else 0
+        for way in range(2):
+            for t in range(hops(n, unit)[way]):
+                block = me.at(-1 - t if way == 0 else 1 + t)
+                here = peer_part(k, block, me.x)
+                remote(
+                    here, here, core_s.at[k, way, t], core_r.at[k, way, t], me.core_peer
+                ).wait_recv()
+                if unit:
+                    here = peer_part(k, block, 1 - me.x)
+                    i = k - 2
+                    remote(
+                        here, here, far_s.at[i, way, t], far_r.at[i, way, t], me.core_peer
+                    ).wait_recv()
+    for j in range(1, n):
+        here = outs[4].at[(me.s + n - j) % n]
+        remote(here, here, small_s.at[j], small_r.at[j], me.core_peer).wait_recv()
+    for copy in pending:
+        copy.wait_send()
+    for copy in own:
+        copy.wait()
+
+
+def gather_weights(n, w_qkv, w_out, w_in, w_back, small):
+    rows = w_qkv.shape[0]
+    w_back = w_back.reshape(4, rows, w_back.shape[1])
+    operands = (w_qkv, w_out, w_in, w_back, small)
+    most = n // 2
+    dma = pltpu.SemaphoreType.DMA
+    full = pl.pallas_call(
+        functools.partial(gather_kernel, n),
+        out_shape=[jax.ShapeDtypeStruct((n,) + a.shape, a.dtype) for a in operands],
+        in_specs=[pl.BlockSpec(memory_space=pl.ANY)] * 5,
+        out_specs=[pl.BlockSpec(memory_space=pl.ANY)] * 5,
+        scratch_shapes=[dma((5,))]
+        + [dma((4, 2, most))] * 2
+        + [dma((2, 2, most))] * 2
+        + [dma((4, 2, most))] * 2
+        + [dma((2, 2, most))] * 2
+        + [dma((n,))] * 2,
+        compiler_params=pltpu.CompilerParams(collective_id=0, has_side_effects=True),
+        name="gather_weights",
+    )(*operands)
+    return (
+        full[0].reshape(-1, full[0].shape[-1]),
+        full[1].reshape(-1, full[1].shape[-1]),
+        full[2].reshape(-1, full[2].shape[-1]),
+        full[3].reshape(-1, full[3].shape[-1]),
+        full[4],
+    )
+
+
+def reduce_kernel(n, *refs):
+    gq, go, gi, gb, gs, oq, oo, oi, ob, osm = refs[:10]
+    (
+        core_a,
+        core_i,
+        core_b,
+        sent_b,
+        chip_b,
+        slot_a,
+        slot_b,
+        last_as,
+        last_ar,
+        last_bs,
+        last_br,
+        small_c,
+        small_x,
+        small_n,
+        core_s,
+        core_r,
+        chip_s,
+        chip_r,
+        ring_s,
+        ring_r,
+        end_s,
+        end_r,
+        small_s,
+        small_r,
+    ) = refs[10:]
+    me = Place(n)
+    c, x = me.c, me.x
+    half_q, half_o = gq.shape[2] // 2, go.shape[2] // 2
+    quarter = gi.shape[2] // 4
+    wide = half_q + half_o
+    f32, bf16 = jnp.float32, jnp.bfloat16
+    pending = []
+
+    def go_remote(*args):
+        copy = remote(*args)
+        copy.start()
+        pending.append(copy)
+
+    me.greet()
+    (more, less) = hops(n, 0)
+    order = []
+    for t in range(more):
+        order.append(more - t)
+        if t < less + 1 and less - t > 0:
+            order.append(-(less - t))
+    order.append(0)
+    order_b = [-o for o in order]
+
+    core = lambda k, src, dst, b: remote(src, dst, core_s.at[k, b], core_r.at[k, b], me.core_peer)
+    for j, o in enumerate(order_b):
+        b = me.at(o)
+        go_remote(gi.at[b, :, cols(1 - c, 2 * quarter)], core_i.at[b], core_s.at[2, j], core_r.at[2, j], me.core_peer)
+        go_remote(gb.at[b, pl.ds((1 - c) * 2, 2)], core_b.at[b], core_s.at[3, j], core_r.at[3, j], me.core_peer)
+    go_remote(gs, small_c, small_s.at[0], small_r.at[0], me.core_peer)
+    for j, o in enumerate(order):
+        b = me.at(o)
+        go_remote(gq.at[b, :, cols(1 - c, half_q)], core_a.at[b, :, pl.ds(0, half_q)], core_s.at[0, j], core_r.at[0, j], me.core_peer)
+        go_remote(go.at[b, :, cols(1 - c, half_o)], core_a.at[b, :, pl.ds(half_q, half_o)], core_s.at[1, j], core_r.at[1, j], me.core_peer)
+
+    def arrived(dst, send, recv):
+        remote(dst, dst, send, recv, me.core_peer).wait_recv()
+
+    for j, o in enumerate(order_b):
+        b = me.at(o)
+        arrived(core_i.at[b], core_s.at[2, j], core_r.at[2, j])
+        arrived(core_b.at[b], core_s.at[3, j], core_r.at[3, j])
+        sent_b[b, :, 0:quarter] = (
+            gi[b, :, cols(c * 2 + 1 - x, quarter)].astype(f32)
+            + core_i[b, :, cols(1 - x, quarter)].astype(f32)
+        ).astype(bf16)
+        sent_b[b, :, quarter : 2 * quarter] = (
+            gb[b, c * 2 + 1 - x].astype(f32) + core_b[b, 1 - x].astype(f32)
+        ).astype(bf16)
+        go_remote(sent_b.at[b], chip_b.at[b], chip_s.at[j], chip_r.at[j], me.chip_peer)
+
+    arrived(small_c, small_s.at[0], small_r.at[0])
+    small_c[...] = small_c[...] + gs[...]
+    go_remote(small_c, small_x, small_s.at[1], small_r.at[1], me.chip_peer)
+
+    def ready_a(j):
+        b = me.at(order[j])
+        arrived(core_a.at[b, :, pl.ds(0, half_q)], core_s.at[0, j], core_r.at[0, j])
+        arrived(core_a.at[b, :, pl.ds(half_q, half_o)], core_s.at[1, j], core_r.at[1, j])
+        core_a[b, :, 0:half_q] = (
+            core_a[b, :, 0:half_q].astype(f32) + gq[b, :, cols(c, half_q)].astype(f32)
+        ).astype(bf16)
+        core_a[b, :, half_q:wide] = (
+            core_a[b, :, half_q:wide].astype(f32) + go[b, :, cols(c, half_o)].astype(f32)
+        ).astype(bf16)
+
+    def ready_b(j):
+        b = me.at(order_b[j])
+        arrived(chip_b.at[b], chip_s.at[j], chip_r.at[j])
+        chip_b[b, :, 0:quarter] = (
+            chip_b[b, :, 0:quarter].astype(f32)
+            + (
+                gi[b, :, cols(c * 2 + x, quarter)].astype(f32)
+                + core_i[b, :, cols(x, quarter)].astype(f32)
+            )
+        ).astype(bf16)
+        chip_b[b, :, quarter : 2 * quarter] = (
+            chip_b[b, :, quarter : 2 * quarter].astype(f32)
+            + (gb[b, c * 2 + x].astype(f32) + core_b[b, x].astype(f32))
+        ).astype(bf16)
+
+    def step(unit, way, t):
+        total = core_a if unit == 0 else chip_b
+        slots = slot_a if unit == 0 else slot_b
+        offsets = order if unit == 0 else order_b
+        count = hops(n, unit)[way]
+        offset = (count - t) if way == 0 else -(count - t)
+        (ready_a if unit == 0 else ready_b)(offsets.index(offset))
+        b = me.at(offset)
+        if t == 0:
+            src = total.at[b]
+        else:
+            arrived(slots.at[way, t - 1], ring_s.at[unit, way, t - 1], ring_r.at[unit, way, t - 1])
+            slots[way, t - 1] = (
+                slots[way, t - 1].astype(f32) + total[b].astype(f32)
+            ).astype(bf16)
+            src = slots.at[way, t - 1]
+        go_remote(
+            src,
+            slots.at[way, t],
+            ring_s.at[unit, way, t],
+            ring_r.at[unit, way, t],
+            me.right if way == 0 else me.left,
+        )
+
+    def steps(unit, t):
+        for way in range(2):
+            if 0 <= t < hops(n, unit)[way]:
+                step(unit, way, t)
+
+    def small_spread():
+        arrived(small_x, small_s.at[1], small_r.at[1])
+        small_x[...] = small_x[...] + small_c[...]
+        for j in range(1, n):
+            other = (me.s + j) % n
+            go_remote(small_x.at[other], small_n.at[me.s], small_s.at[1 + j], small_r.at[1 + j], (other, me.r))
+
+    def finish(unit):
+        total = core_a if unit == 0 else chip_b
+        slots = slot_a if unit == 0 else slot_b
+        (ready_a if unit == 0 else ready_b)(n - 1)
+        acc = total[me.s].astype(f32)
+        for way in range(2):
+            last = hops(n, unit)[way] - 1
+            arrived(slots.at[way, last], ring_s.at[unit, way, last], ring_r.at[unit, way, last])
+            acc = acc + slots[way, last].astype(f32)
+        (last_as if unit == 0 else last_bs)[...] = acc.astype(bf16)
+        if unit == 0:
+            go_remote(last_as, last_ar, end_s.at[0], end_r.at[0], me.chip_peer)
+        else:
+            go_remote(last_bs, last_br, end_s.at[1], end_r.at[1], me.chip_peer)
+
+    for t in range(more + 1):
+        steps(0, t)
+        if t == 0:
+            small_spread()
+        if t == more:
+            finish(0)
+        steps(1, t - 1)
+    finish(1)
+    arrived(last_ar, end_s.at[0], end_r.at[0])
+    both = last_as[...].astype(f32) + last_ar[...].astype(f32)
+    oq[:, cols(c, half_q)] = both[:, 0:half_q]
+    oo[:, cols(c, half_o)] = both[:, half_q:wide]
+    for k, ref, width in ((2, oq, half_q), (3, oo, half_o)):
+        place = ref.at[:, cols(c, width)]
+        go_remote(place, place, end_s.at[k], end_r.at[k], me.core_peer)
+    acc = last_bs[...].astype(f32)
+    oi[:, cols(c * 2 + x, quarter)] = acc[:, 0:quarter]
+    ob[c * 2 + x] = acc[:, quarter : 2 * quarter]
+    small_n[me.s] = small_x[me.s]
+    for j in range(1, n):
+        arrived(small_n.at[(me.s + n - j) % n], small_s.at[1 + j], small_r.at[1 + j])
+    acc = small_n[0]
+    for j in range(1, n):
+        acc = acc + small_n[j]
+    osm[...] = acc
+    arrived(last_br, end_s.at[1], end_r.at[1])
+    acc = last_br[...].astype(f32)
+    oi[:, cols(c * 2 + 1 - x, quarter)] = acc[:, 0:quarter]
+    ob[c * 2 + 1 - x] = acc[:, quarter : 2 * quarter]
+    place = oi.at[:, cols(c, 2 * quarter)]
+    go_remote(place, place, end_s.at[4], end_r.at[4], me.core_peer)
+    place = ob.at[pl.ds(c * 2, 2)]
+    go_remote(place, place, end_s.at[5], end_r.at[5], me.core_peer)
+    for k, ref, width in ((2, oq, half_q), (3, oo, half_o), (4, oi, 2 * quarter)):
+        arrived(ref.at[:, cols(1 - c, width)], end_s.at[k], end_r.at[k])
+    arrived(ob.at[pl.ds((1 - c) * 2, 2)], end_s.at[5], end_r.at[5])
+    for copy in pending:
+        copy.wait_send()
+
+
+def reduce_gradients(n, d_qkv, d_out, d_in, d_back, small):
+    rows = d_qkv.shape[0] // n
+    bf16, f32 = jnp.bfloat16, jnp.float32
+    operands = (
+        d_qkv.reshape(n, rows, -1),
+        d_out.reshape(n, rows, -1),
+        d_in.reshape(n, rows, -1),
+        d_back.reshape(n, 4, rows, -1),
+        small,
+    )
+    quarter = d_in.shape[1] // 4
+    wide = (d_qkv.shape[1] + d_out.shape[1]) // 2
+    most = n // 2
+    dma = pltpu.SemaphoreType.DMA
+    vmem = pltpu.VMEM
+    block = (rows, wide)
+    outs = pl.pallas_call(
+        functools.partial(reduce_kernel, n),
+        out_shape=[jax.ShapeDtypeStruct(a.shape[1:], f32) for a in operands],
+        in_specs=[pl.BlockSpec(memory_space=pltpu.VMEM)] * 5,
+        out_specs=[pl.BlockSpec(memory_space=pltpu.VMEM)] * 5,
+        scratch_shapes=[
+            vmem((n,) + block, bf16),
+            vmem((n, rows, 2 * quarter), bf16),
+            vmem((n, 2, rows, quarter), bf16),
+            vmem((n, rows, 2 * quarter), bf16),
+            vmem((n, rows, 2 * quarter), bf16),
+            vmem((2, most) + block, bf16),
+            vmem((2, most, rows, 2 * quarter), bf16),
+            vmem(block, bf16),
+            vmem(block, bf16),
+            vmem((rows, 2 * quarter), bf16),
+            vmem((rows, 2 * quarter), bf16),
+            vmem(small.shape, f32),
+            vmem(small.shape, f32),
+            vmem(small.shape, f32),
+            dma((4, n)),
+            dma((4, n)),
+            dma((n,)),
+            dma((n,)),
+            dma((2, 2, most)),
+            dma((2, 2, most)),
+            dma((6,)),
+            dma((6,)),
+            dma((n + 1,)),
+            dma((n + 1,)),
+        ],
+        compiler_params=pltpu.CompilerParams(
+            collective_id=1, has_side_effects=True, vmem_limit_bytes=50 * 2**20
+        ),
+        name="reduce_gradients",
+    )(*operands)
+    outs = list(outs)
+    outs[3] = outs[3].reshape(4 * rows, -1)
+    return outs
+
+
+def pack_small(parts, n):
+    joined = jnp.concatenate([v.reshape(n, -1) for v in parts], 1)
+    width = joined.shape[1]
+    padded = -(-width // 2048) * 2048
+    joined = jnp.pad(joined, ((0, 0), (0, padded - width)))
+    return joined.reshape(n, padded // 128, 128)
+
+
+def unpack_small(packed, sizes):
+    flat = packed.reshape(packed.shape[0], -1)
+    result, start = [], 0
+    for size in sizes:
+        result.append(flat[:, start : start + size].reshape(-1))
+        start += size
+    return result
 
 
 def normalize(summed, gain_row, shift_row):
@@ -36,6 +518,8 @@
 
 
 def body(
+    n_shard,
+    n_rep,
     tokens,
     labels,
     w_qkv,
@@ -52,34 +536,30 @@
     shift_two,
     cotangent,
 ):
-    gathered = (
-        lax.all_gather(w_qkv, "shard", axis=0, tiled=True),
-        lax.all_gather(bias_qv, "shard", axis=0, tiled=True),
-        lax.all_gather(w_out, "shard", axis=0, tiled=True),
-        lax.all_gather(bias_out, "shard", axis=0, tiled=True),
-        lax.all_gather(w_in, "shard", axis=0, tiled=True),
-        lax.all_gather(bias_in, "shard", axis=0, tiled=True),
-        lax.all_gather(w_back, "shard", axis=0, tiled=True),
-        lax.all_gather(bias_back, "shard", axis=0, tiled=True),
-        lax.all_gather(gain_one, "shard", axis=0, tiled=True),
-        lax.all_gather(shift_one, "shard", axis=0, tiled=True),
-        lax.all_gather(gain_two, "shard", axis=0, tiled=True),
-        lax.all_gather(shift_two, "shard", axis=0, tiled=True),
+    vectors = (
+        bias_qv,
+        bias_out,
+        bias_in,
+        bias_back,
+        gain_one,
+        shift_one,
+        gain_two,
+        shift_two,
+    )
+    sizes = [v.shape[0] for v in vectors]
+    full_qkv, full_out, full_in, full_back, packed = gather_weights(
+        n_shard, w_qkv, w_out, w_in, w_back, pack_small(vectors, 1)[0]
     )
     (
-        full_qkv,
         full_bias_qv,
-        full_out,
         full_bias_out,
-        full_in,
         full_bias_in,
-        full_back,
         full_bias_back,
         full_gain_one,
         full_shift_one,
         full_gain_two,
         full_shift_two,
-    ) = gathered
+    ) = unpack_small(packed, sizes)
     model_width = full_out.shape[0]
     row_count = tokens.shape[0]
     score_scale = 1.0 / math.sqrt(HEAD_DIM)
@@ -122,45 +602,31 @@
     final_out, unit_two, scale_two = normalize(first_out + branch, full_gain_two, full_shift_two)
     live_rows = (labels > 0).astype(jnp.float32)[:, None]
     output = (final_out * live_rows).astype(jnp.bfloat16)
-    (
-        back_qkv,
-        unused_bias_qv,
-        back_out,
-        unused_bias_out,
-        back_in,
-        unused_bias_in,
-        back_weights,
-        unused_bias_back,
-        back_gain_one,
-        unused_shift_one,
-        back_gain_two,
-        unused_shift_two,
-    ) = gathered
     grad_final = cotangent.astype(jnp.float32) * live_rows
     d_gain_two = jnp.sum(grad_final * unit_two, 0)
     d_shift_two = jnp.sum(grad_final, 0)
-    grad_mid = norm_back(grad_final * back_gain_two.astype(jnp.float32), unit_two, scale_two)
+    grad_mid = norm_back(grad_final * full_gain_two.astype(jnp.float32), unit_two, scale_two)
     grad_branch = grad_mid.astype(jnp.bfloat16)
     d_w_back = jnp.einsum("tf,td->fd", activated, grad_branch, preferred_element_type=jnp.float32)
     d_bias_back = jnp.sum(grad_branch.astype(jnp.float32), 0)
     grad_act = jnp.einsum(
-        "td,fd->tf", grad_branch, back_weights, preferred_element_type=jnp.float32
+        "td,fd->tf", grad_branch, full_back, preferred_element_type=jnp.float32
     )
     unused_value, gelu_pull = jax.vjp(gelu_exact, inner_sum)
     grad_inner = gelu_pull(grad_act)[0].astype(jnp.bfloat16)
     d_w_in = jnp.einsum("td,tf->df", first_low, grad_inner, preferred_element_type=jnp.float32)
     d_bias_in = jnp.sum(grad_inner.astype(jnp.float32), 0)
     grad_first = (
-        jnp.einsum("tf,df->td", grad_inner, back_in, preferred_element_type=jnp.float32) + grad_mid
+        jnp.einsum("tf,df->td", grad_inner, full_in, preferred_element_type=jnp.float32) + grad_mid
     )
     d_gain_one = jnp.sum(grad_first * unit_one, 0)
     d_shift_one = jnp.sum(grad_first, 0)
-    grad_res = norm_back(grad_first * back_gain_one.astype(jnp.float32), unit_one, scale_one)
+    grad_res = norm_back(grad_first * full_gain_one.astype(jnp.float32), unit_one, scale_one)
     grad_attn = grad_res.astype(jnp.bfloat16)
     d_w_out = jnp.einsum("td,te->de", mixed_heads, grad_attn, preferred_element_type=jnp.float32)
     d_bias_out = jnp.sum(grad_attn.astype(jnp.float32), 0)
     grad_mixed = jnp.einsum(
-        "te,de->td", grad_attn, back_out, preferred_element_type=jnp.float32
+        "te,de->td", grad_attn, full_out, preferred_element_type=jnp.float32
     ).astype(jnp.bfloat16)
     grad_mixed_heads = grad_mixed.reshape(row_count, HEADS, HEAD_DIM)
     grad_attention = jnp.einsum(
@@ -188,54 +654,42 @@
         [jnp.sum(grad_query.astype(jnp.float32), 0), jnp.sum(grad_values.astype(jnp.float32), 0)], 0
     )
     grad_tokens = (
-        jnp.einsum("te,de->td", grad_qkv, back_qkv, preferred_element_type=jnp.float32) + grad_res
-    )
-    owned = (
-        lax.psum_scatter(d_w_qkv, "shard", scatter_dimension=0, tiled=True),
-        lax.psum_scatter(d_bias_qv, "shard", scatter_dimension=0, tiled=True),
-        lax.psum_scatter(d_w_out, "shard", scatter_dimension=0, tiled=True),
-        lax.psum_scatter(d_bias_out, "shard", scatter_dimension=0, tiled=True),
-        lax.psum_scatter(d_w_in, "shard", scatter_dimension=0, tiled=True),
-        lax.psum_scatter(d_bias_in, "shard", scatter_dimension=0, tiled=True),
-        lax.psum_scatter(d_w_back, "shard", scatter_dimension=0, tiled=True),
-        lax.psum_scatter(d_bias_back, "shard", scatter_dimension=0, tiled=True),
-        lax.psum_scatter(d_gain_one, "shard", scatter_dimension=0, tiled=True),
-        lax.psum_scatter(d_shift_one, "shard", scatter_dimension=0, tiled=True),
-        lax.psum_scatter(d_gain_two, "shard", scatter_dimension=0, tiled=True),
-        lax.psum_scatter(d_shift_two, "shard", scatter_dimension=0, tiled=True),
-    )
-    summed = lax.psum(
+        jnp.einsum("te,de->td", grad_qkv, full_qkv, preferred_element_type=jnp.float32) + grad_res
+    )
+    low_grads = [g.astype(jnp.bfloat16) for g in (d_w_qkv, d_w_out, d_w_in, d_w_back)]
+    small_grads = pack_small(
         (
-            owned[0],
-            owned[1],
-            owned[2],
-            owned[3],
-            owned[4],
-            owned[5],
-            owned[6],
-            owned[7],
-            owned[8],
-            owned[9],
-            owned[10],
-            owned[11],
+            d_bias_qv,
+            d_bias_out,
+            d_bias_in,
+            d_bias_back,
+            d_gain_one,
+            d_shift_one,
+            d_gain_two,
+            d_shift_two,
         ),
-        "rep",
-    )
+        n_shard,
+    )
+    summed = reduce_gradients(n_shard, *low_grads, small_grads)
+    if n_rep > QUAD:
+        summed = [lax.psum(g, "rep") * (1.0 / QUAD) for g in summed]
+    d_qkv, d_out, d_in, d_back, packed = summed
+    vector = unpack_small(packed[None], sizes)
     return (
         output,
         grad_tokens,
-        summed[0],
-        summed[1],
-        summed[2],
-        summed[3],
-        summed[4],
-        summed[5],
-        summed[6],
-        summed[7],
-        summed[8],
-        summed[9],
-        summed[10],
-        summed[11],
+        d_qkv,
+        vector[0],
+        d_out,
+        vector[1],
+        d_in,
+        vector[2],
+        d_back,
+        vector[3],
+        vector[4],
+        vector[5],
+        vector[6],
+        vector[7],
     )
 
 
@@ -258,7 +712,7 @@
         P(("shard", "rep"), None),
     )
     return jax.shard_map(
-        body,
+        functools.partial(body, mesh.shape["shard"], mesh.shape["rep"]),
         mesh=mesh,
         in_specs=placed,
         out_specs=(

time: 941 us -> 254 us (0.27)
  waiting for transfers between devices: 730 us -> 0 us
  Pallas kernels: 0 us -> 179 us
  blocking collectives: 109 us -> 0 us
  between operations: 17.9 us -> 1.24 us
    reduce_scatter x3 -> x0, waiting for transfers between devices: 402 us -> none  [the longest x1 166 us: body(): lax.psum_scatter(d_w_back, 'shard', scatter_dimension=0, tiled=True)]
    all_gather x4 -> x0, waiting for transfers between devices: 187 us -> none  [the longest x1 78.9 us: body(): lax.all_gather(w_in, 'shard', axis=0, tiled=True)]
    pallas_call x0 -> x2, Pallas kernels: none -> 179 us  [the longest x1 116 us: reduce_gradients(): pl.pallas_call(functools.partial(reduce_kernel, n), out_shape=[jax.ShapeD...]
    unnamed x10 -> x0, waiting for transfers between devices: 117 us -> none
    unnamed x2 -> x0, blocking collectives: 76.2 us -> none
    all_gather x1 -> x0, blocking collectives: 26.1 us -> none  [body(): lax.all_gather(bias_in, 'shard', axis=0, tiled=True)]
    psum x1 -> x0, waiting for transfers between devices: 24.7 us -> none  [body(): lax.psum((owned[0], owned[1], owned[2], owned[3], owned[4], owned[5], own...]
    unnamed x108 -> x99, local copies, waits for them, and re-layouts: 28.3 us -> 6.98 us
  transfers between devices with their start and end apart: 9 -> 0, of which waited for: 8 -> 0; matrix products, arithmetic and copies ran while one was open for 5% -> 0% of each run, Pallas kernels for 0% -> 0%
where the time goes in v1:
time: 254 us
  Pallas kernels  179 us (70%)
  matrix products  42.9 us (17%)
  local copies, waits for them, and re-layouts  21.8 us (9%)
  other arithmetic  8.94 us (4%)
    pallas_call x1, Pallas kernels, reduce_gradients(): pl.pallas_call(functools.partial(reduce_kernel, n), out_shape=[jax.ShapeD...  116 us
    pallas_call x1, Pallas kernels, gather_weights(): pl.pallas_call(functools.partial(gather_kernel, n), out_shape=[jax.ShapeD...  62.8 us
    dot_general x1, matrix products, body(): jnp.dot(first_low, full_in, preferred_element_type=jnp.float32)  8.9 us
    reshape x9, local copies, waits for them, and re-layouts, pack_small(): joined = jnp.concatenate([v.reshape(n, -1) for v in parts], 1)  7.28 us
    unnamed x99, local copies, waits for them, and re-layouts  6.98 us
    dot_general x1, matrix products, body(): jnp.einsum('td,fd->tf', grad_branch, full_back, preferred_element_type=jn...  5.17 us

profile of v1, /device:TPU:0, one launch (start us, length us, event | category | flops | bytes accessed | tf_op | source)
XLA Modules:
  0.0 253.8 jit_solution(1623650076684727145)
XLA Ops:
  0.7 1.2 compare_convert_fusion
  5.5 62.8 %gather_weights.1 = (bf16[8,96,2304]{2,1,0:T(8,128)(2,1)}, bf16[8,96,768]{2,1,0:T(8,128)(2,1)}, bf16[8,96,3072]{2,1,0:T(8,128)(2,1)}, bf16[8,4,96,768]{3,2,1,0:T(8,128)(2,1)}, bf16[8,16,128]{2,1,0:T(8,128)(2,1)}) custom-call(bf16[96,2304]{1,0:T(8,128)(2,1)} %refs_0_.1, bf16[96,768]{1,0:T(8,128)(2,1)} %refs_1_.1, bf16[96,3072]{1,0:T(8,128)(2,1)} %refs_2_.1, ...), custom_call_target="tpu_custom_call" | custom-call | tf_op jit(solution)/shard_map/gather_weights/pallas_call | solution.py:201
  71.1 3.1 %convolution_bitcast_fusion = f32[128,2304]{0,1:T(8,128)S(1)} fusion(bf16[768,2304]{1,0:T(8,128)(2,1)} %bitcast.99, bf16[128,768]{1,0:T(8,128)(2,1)S(1)} %copy-done.11), kind=kOutput, calls=%fused_computation.4 | convolution fusion | flops 452984832 | bytes 4915200 | tf_op jit(solution)/shard_map/dot_general | solution.py:566
  75.6 0.9 copy-done.6
  77.3 8.9 %multiply_convert_fusion = (bf16[128,3072]{1,0:T(8,128)(2,1)S(1)}, f32[128,3072]{1,0:T(8,128)}, f32[128,3072]{1,0:T(8,128)}) fusion(f32[3072]{0:T(1024)S(1)} %reshape.342, bf16[768,3072]{1,0:T(8,128)(2,1)} %bitcast.109, f32[128,768]{1,0:T(8,128)S(1)} %get-tuple-element.68, f32[768]{0:T(1024)S(1)} %reshape.341, f32[768]{0:T(1024)S(1)} %reshape.340, ...), kind=kOutput, calls=%fused_computation.10 | convolution fusion | flops 630423552 | bytes 9063424 | tf_op jit(solution)/shard_map/dot_general | solution.py:595
  88.6 1.4 reshape.327
  89.9 1.2 broadcast_multiply_fusion.2
  91.1 1.3 reshape.328
  92.5 2.4 convert_reduce_fusion.1
  94.9 5.2 %convert_reduce_fusion = (f32[3072]{0:T(1024)S(1)}, bf16[128,3072]{1,0:T(8,128)(2,1)S(1)}) fusion(f32[128,3072]{1,0:T(8,128)} %get-tuple-element.47, f32[128,3072]{1,0:T(8,128)} %get-tuple-element.69, bf16[3072,768]{1,0:T(8,128)(2,1)} %bitcast.103, f32[128,768]{1,0:T(8,128)S(1)} %get-tuple-element.43), kind=kOutput, calls=%fused_computation.8 | convolution fusion | flops 610366464 | bytes 9056256 | tf_op jit(solution)/shard_map/td,fd->tf/dot_general | solution.py:612
  100.1 2.4 multiply_reduce_fusion.2
  107.5 2.1 convert_reduce_fusion.3
  110.9 1.4 multiply_convert_fusion.1
  112.3 1.0 fusion.13
  113.4 0.9 convert_reduce_fusion.4
  115.0 3.3 %convolution_add_fusion.2 = f32[128,768]{1,0:T(8,128)} fusion(f32[128,768]{1,0:T(8,128)} %copy-done.3, bf16[768,2304]{1,0:T(8,128)(2,1)S(1)} %bitcast.100, bf16[128,768]{0,1:T(8,128)(2,1)} %bitcast.117, bf16[128,768]{0,1:T(8,128)(2,1)} %bitcast.113, bf16[128,768]{0,1:T(8,128)(2,1)} %bitcast.115), kind=kOutput, calls=%fused_computation.31 | convolution fusion | flops 454852608 | bytes 4915200 | tf_op jit(solution)/shard_map/te,de->td/dot_general | solution.py:657
  119.3 2.6 %convolution_convert_fusion.3 = bf16[768,768]{1,0:T(8,128)(2,1)} fusion(bf16[128,768]{0,1:T(8,128)(2,1)} %bitcast.120, f32[128,768]{1,0:T(8,128)} %copy-done.3), kind=kOutput, calls=%fused_computation.24 | convolution fusion | flops 151683072 | bytes 1769472 | tf_op jit(solution)/shard_map/td,te->de/dot_general | solution.py:626
  122.0 2.9 %convolution_convert_fusion.2 = bf16[2304,768]{0,1:T(8,128)(2,1)} fusion(bf16[128,768]{1,0:T(8,128)(2,1)S(1)} %copy-done.12, bf16[128,768]{0,1:T(8,128)(2,1)S(1)} %bitcast.118, bf16[128,768]{0,1:T(8,128)(2,1)S(1)} %bitcast.114, bf16[128,768]{0,1:T(8,128)(2,1)S(1)} %bitcast.116), kind=kOutput, calls=%fused_computation.3 | convolution fusion | flops 456523776 | bytes 4325376 | tf_op jit(solution)/shard_map/td,te->de/dot_general | solution.py:652
  124.9 3.6 %convolution_convert_fusion.1 = bf16[768,3072]{1,0:T(8,128)(2,1)} fusion(bf16[128,3072]{1,0:T(8,128)(2,1)S(1)} %copy-done.10, f32[128,768]{1,0:T(8,128)S(1)} %copy-done.2, f32[768]{0:T(1024)S(1)} %reshape.341, f32[768]{0:T(1024)S(1)} %reshape.340, f32[128]{0:T(128)S(1)} %copy-done.35, f32[128]{0:T(128)S(1)} %copy-done.24), kind=kOutput, calls=%fused_computation.2 | convolution fusion | flops 606830592 | bytes 5905408 | tf_op jit(solution)/shard_map/td,tf->df/dot_general | solution.py:617
  128.5 3.6 %convolution_convert_fusion = bf16[3072,768]{1,0:T(8,128)(2,1)} fusion(bf16[128,3072]{1,0:T(8,128)(2,1)S(1)} %copy-done.5, f32[128,768]{1,0:T(8,128)S(1)} %copy-done.8), kind=kOutput, calls=%fused_computation.1 | convolution fusion | flops 606437376 | bytes 5898240 | tf_op jit(solution)/shard_map/tf,td->fd/dot_general | solution.py:610
  132.1 116.2 %reduce_gradients.1 = (f32[96,2304]{1,0:T(8,128)S(1)}, f32[96,768]{1,0:T(8,128)S(1)}, f32[96,3072]{1,0:T(8,128)S(1)}, f32[4,96,768]{2,1,0:T(8,128)S(1)}, f32[16,128]{1,0:T(8,128)S(1)}) custom-call(bf16[8,96,2304]{2,1,0:T(8,128)(2,1)} %bitcast.101, bf16[8,96,768]{2,1,0:T(8,128)(2,1)} %bitcast.102, bf16[8,96,3072]{2,1,0:T(8,128)(2,1)} %bitcast.97, ...), custom_call_target="tpu_custom_call" | custom-call | tf_op jit(solution)/shard_map/reduce_gradients/pallas_call | solution.py:439
  250.1 0.9 copy.54
  251.8 1.0 copy.56
  252.8 1.0 copy.57
  (146 shorter events, 21.2 us)
Async XLA Ops:
  0.6 70.4 %copy-start.11 = (bf16[128,768]{1,0:T(8,128)(2,1)S(1)}, bf16[128,768]{1,0:T(8,128)(2,1)}, u32[]{:S(2)}) copy-start(bf16[128,768]{1,0:T(8,128)(2,1)} %param.15) | copy-start | bytes 589828
  5.5 69.5 %copy-start.29 = (pred[128,128]{0,1:T(8,128)(4,1)}, pred[128,128]{0,1:T(8,128)(4,1)S(1)}, u32[]{:S(2)}) copy-start(pred[128,128]{0,1:T(8,128)(4,1)S(1)} %broadcast_compare_fusion) | copy-start | bytes 49156
  74.2 33.2 %copy-start.19 = (bf16[128,768]{0,1:T(8,128)(2,1)}, bf16[128,768]{0,1:T(8,128)(2,1)S(1)}, u32[]{:S(2)}) copy-start(bf16[128,768]{0,1:T(8,128)(2,1)S(1)} %slice.136) | copy-start | bytes 589828
  74.5 33.0 %copy-start.17 = (bf16[128,768]{0,1:T(8,128)(2,1)}, bf16[128,768]{0,1:T(8,128)(2,1)S(1)}, u32[]{:S(2)}) copy-start(bf16[128,768]{0,1:T(8,128)(2,1)S(1)} %get-tuple-element.48) | copy-start | bytes 589828
  75.0 35.2 %copy-start.21 = (f32[12,128,128]{1,2,0:T(8,128)}, f32[12,128,128]{1,2,0:T(8,128)S(1)}, u32[]{:S(2)}) copy-start(f32[12,128,128]{1,2,0:T(8,128)S(1)} %get-tuple-element.66) | copy-start | bytes 2359300
  75.6 10.5 %copy-start.16 = (bf16[12,64,128]{2,1,0:T(8,128)(2,1)}, bf16[12,64,128]{2,1,0:T(8,128)(2,1)S(1)}, u32[]{:S(2)}) copy-start(bf16[12,64,128]{2,1,0:T(8,128)(2,1)S(1)} %convolution_convert_fusion.6) | copy-start | bytes 589828
  76.5 9.6 %slice-start = ((s8[4718592]{0:T(1024)(128)(4,1)}), s8[4194304]{0:T(1024)(128)(4,1)S(1)}, s32[]{:S(2)}) async-start(s8[4718592]{0:T(1024)(128)(4,1)} %bitcast.104), calls=%async_computation | async-start | bytes 8388608
  77.0 27.4 %copy-start.1 = (f32[128,768]{1,0:T(8,128)}, f32[128,768]{1,0:T(8,128)S(1)}, u32[]{:S(2)}) copy-start(f32[128,768]{1,0:T(8,128)S(1)} %get-tuple-element.68) | copy-start | bytes 1179652
  77.0 27.4 %copy-start.23 = (f32[128]{0:T(128)}, f32[128]{0:T(128)S(1)}, u32[]{:S(2)}) copy-start(f32[128]{0:T(128)S(1)} %broadcast_multiply_fusion.5) | copy-start | bytes 1540
  77.2 8.9 %copy-start.33 = (f32[128]{0:T(128)}, f32[128]{0:T(128)S(1)}, u32[]{:S(2)}) copy-start(f32[128]{0:T(128)S(1)} %add_rsqrt_fusion.1) | copy-start | bytes 1540
  77.2 8.9 %slice-start.1 = ((s8[4718592]{0:T(1024)(128)(4,1)}), s8[524288]{0:T(1024)(128)(4,1)S(1)}, s32[]{:S(2)}) async-start(s8[4718592]{0:T(1024)(128)(4,1)} %bitcast.104), calls=%async_computation.1 | async-start | bytes 1048576
  77.2 8.9 %copy-start.25 = (f32[768]{0:T(1024)S(1)}, f32[768]{0:T(1024)}, u32[]{:S(2)}) copy-start(f32[768]{0:T(1024)} %reshape.343) | copy-start | bytes 9220
  92.5 7.6 %slice-start.2 = ((s8[4718592]{0:T(1024)(128)(4,1)}), s8[4194304]{0:T(1024)(128)(4,1)S(1)}, s32[]{:S(2)}) async-start(s8[4718592]{0:T(1024)(128)(4,1)} %bitcast.110), calls=%async_computation.2 | async-start | bytes 8388608
  94.9 5.2 %copy-start.7 = (f32[128,768]{1,0:T(8,128)}, f32[128,768]{1,0:T(8,128)S(1)}, u32[]{:S(2)}) copy-start(f32[128,768]{1,0:T(8,128)S(1)} %get-tuple-element.43) | copy-start | bytes 1179652
  94.9 5.2 %slice-start.3 = ((s8[4718592]{0:T(1024)(128)(4,1)}), s8[524288]{0:T(1024)(128)(4,1)S(1)}, s32[]{:S(2)}) async-start(s8[4718592]{0:T(1024)(128)(4,1)} %bitcast.110), calls=%async_computation.3 | async-start | bytes 1048576
  94.9 5.2 %copy-start.34 = (f32[128]{0:T(128)S(1)}, f32[128]{0:T(128)}, u32[]{:S(2)}) copy-start(f32[128]{0:T(128)} %copy-done.33) | copy-start | bytes 1540
  100.1 3.6 %copy-start.26 = (f32[768]{0:T(1024)S(1)}, f32[768]{0:T(1024)}, u32[]{:S(2)}) copy-start(f32[768]{0:T(1024)} %get-tuple-element.42) | copy-start | bytes 9220
  110.9 4.1 %copy-start = (bf16[8,96,2304]{2,1,0:T(8,128)(2,1)S(1)}, bf16[8,96,2304]{2,1,0:T(8,128)(2,1)}, u32[]{:S(2)}) copy-start(bf16[8,96,2304]{2,1,0:T(8,128)(2,1)} %get-tuple-element.24) | copy-start | bytes 10616836
  118.3 3.6 %copy-start.12 = (bf16[128,768]{1,0:T(8,128)(2,1)S(1)}, bf16[128,768]{1,0:T(8,128)(2,1)}, u32[]{:S(2)}) copy-start(bf16[128,768]{1,0:T(8,128)(2,1)} %param.15) | copy-start | bytes 589828
  118.3 3.6 %copy-start.13 = (bf16[12,64,128]{2,1,0:T(8,128)(2,1)S(1)}, bf16[12,64,128]{2,1,0:T(8,128)(2,1)}, u32[]{:S(2)}) copy-start(bf16[12,64,128]{2,1,0:T(8,128)(2,1)} %fusion.13) | copy-start | bytes 589828
  118.3 3.6 %copy-start.14 = (bf16[12,64,128]{2,1,0:T(8,128)(2,1)S(1)}, bf16[12,64,128]{2,1,0:T(8,128)(2,1)}, u32[]{:S(2)}) copy-start(bf16[12,64,128]{2,1,0:T(8,128)(2,1)} %get-tuple-element.78) | copy-start | bytes 589828
  118.3 3.6 %copy-start.15 = (bf16[12,64,128]{2,1,0:T(8,128)(2,1)S(1)}, bf16[12,64,128]{2,1,0:T(8,128)(2,1)}, u32[]{:S(2)}) copy-start(bf16[12,64,128]{2,1,0:T(8,128)(2,1)} %get-tuple-element.76) | copy-start | bytes 589828
  124.9 3.7 %copy-start.5 = (bf16[128,3072]{1,0:T(8,128)(2,1)S(1)}, bf16[128,3072]{1,0:T(8,128)(2,1)}, u32[]{:S(2)}) copy-start(bf16[128,3072]{1,0:T(8,128)(2,1)} %copy-done.4) | copy-start | bytes 2359300
  124.9 3.7 %copy-start.8 = (f32[128,768]{1,0:T(8,128)S(1)}, f32[128,768]{1,0:T(8,128)}, u32[]{:S(2)}) copy-start(f32[128,768]{1,0:T(8,128)} %copy-done.7) | copy-start | bytes 1179652
  (22 other events, 46.9 us)

commit v2 on v1

--- a/solution.py
+++ b/solution.py
@@ -222,10 +222,11 @@
 
 
 def reduce_kernel(n, *refs):
-    gq, go, gi, gb, gs, oq, oo, oi, ob, osm = refs[:10]
+    tok, mix, fst, act, gqkv, gattn, ginner, gbranch, gs, oq, oo, oi, ob, osm = refs[:14]
     (
+        out_a,
+        out_b,
         core_a,
-        core_i,
         core_b,
         sent_b,
         chip_b,
@@ -248,11 +249,11 @@
         end_r,
         small_s,
         small_r,
-    ) = refs[10:]
+    ) = refs[14:]
     me = Place(n)
     c, x = me.c, me.x
-    half_q, half_o = gq.shape[2] // 2, go.shape[2] // 2
-    quarter = gi.shape[2] // 4
+    half_q, half_o = gqkv.shape[1] // 2, gattn.shape[1] // 2
+    quarter = ginner.shape[1] // 4
     wide = half_q + half_o
     f32, bf16 = jnp.float32, jnp.bfloat16
     pending = []
@@ -272,32 +273,60 @@
     order.append(0)
     order_b = [-o for o in order]
 
-    core = lambda k, src, dst, b: remote(src, dst, core_s.at[k, b], core_r.at[k, b], me.core_peer)
-    for j, o in enumerate(order_b):
-        b = me.at(o)
-        go_remote(gi.at[b, :, cols(1 - c, 2 * quarter)], core_i.at[b], core_s.at[2, j], core_r.at[2, j], me.core_peer)
-        go_remote(gb.at[b, pl.ds((1 - c) * 2, 2)], core_b.at[b], core_s.at[3, j], core_r.at[3, j], me.core_peer)
-    go_remote(gs, small_c, small_s.at[0], small_r.at[0], me.core_peer)
-    for j, o in enumerate(order):
-        b = me.at(o)
-        go_remote(gq.at[b, :, cols(1 - c, half_q)], core_a.at[b, :, pl.ds(0, half_q)], core_s.at[0, j], core_r.at[0, j], me.core_peer)
-        go_remote(go.at[b, :, cols(1 - c, half_o)], core_a.at[b, :, pl.ds(half_q, half_o)], core_s.at[1, j], core_r.at[1, j], me.core_peer)
+    def product(left, right):
+        return jnp.dot(left, right, preferred_element_type=f32)
+
+    def grad_a(b, core):
+        return (
+            product(tok[b], gqkv[:, cols(core, half_q)]),
+            product(mix[b], gattn[:, cols(core, half_o)]),
+        )
+
+    def grad_b(b, q):
+        return (
+            product(fst[b], ginner[:, cols(q, quarter)]),
+            product(act[b, q], gbranch[...]),
+        )
+
+    def send_b(j):
+        b = me.at(order_b[j])
+        for chip in range(2):
+            first, second = grad_b(b, (1 - c) * 2 + chip)
+            out_b[b, chip, :, 0:quarter] = first.astype(bf16)
+            out_b[b, chip, :, quarter : 2 * quarter] = second.astype(bf16)
+        go_remote(out_b.at[b], core_b.at[b], core_s.at[1, j], core_r.at[1, j], me.core_peer)
+
+    def send_a(j):
+        b = me.at(order[j])
+        first, second = grad_a(b, 1 - c)
+        out_a[b, :, 0:half_q] = first.astype(bf16)
+        out_a[b, :, half_q:wide] = second.astype(bf16)
+        go_remote(out_a.at[b], core_a.at[b], core_s.at[0, j], core_r.at[0, j], me.core_peer)
 
     def arrived(dst, send, recv):
         remote(dst, dst, send, recv, me.core_peer).wait_recv()
 
-    for j, o in enumerate(order_b):
-        b = me.at(o)
-        arrived(core_i.at[b], core_s.at[2, j], core_r.at[2, j])
-        arrived(core_b.at[b], core_s.at[3, j], core_r.at[3, j])
+    def send_chip(j):
+        b = me.at(order_b[j])
+        arrived(core_b.at[b], core_s.at[1, j], core_r.at[1, j])
+        first, second = grad_b(b, c * 2 + 1 - x)
         sent_b[b, :, 0:quarter] = (
-            gi[b, :, cols(c * 2 + 1 - x, quarter)].astype(f32)
-            + core_i[b, :, cols(1 - x, quarter)].astype(f32)
+            first + core_b[b, 1 - x, :, 0:quarter].astype(f32)
         ).astype(bf16)
         sent_b[b, :, quarter : 2 * quarter] = (
-            gb[b, c * 2 + 1 - x].astype(f32) + core_b[b, 1 - x].astype(f32)
+            second + core_b[b, 1 - x, :, quarter : 2 * quarter].astype(f32)
         ).astype(bf16)
         go_remote(sent_b.at[b], chip_b.at[b], chip_s.at[j], chip_r.at[j], me.chip_peer)
+
+    ahead = 2
+    for j in range(n + ahead):
+        if j < n:
+            send_b(j)
+        if j == 0:
+            go_remote(gs, small_c, small_s.at[0], small_r.at[0], me.core_peer)
+        if j >= ahead:
+            send_chip(j - ahead)
+            send_a(j - ahead)
 
     arrived(small_c, small_s.at[0], small_r.at[0])
     small_c[...] = small_c[...] + gs[...]
@@ -305,28 +334,20 @@
 
     def ready_a(j):
         b = me.at(order[j])
-        arrived(core_a.at[b, :, pl.ds(0, half_q)], core_s.at[0, j], core_r.at[0, j])
-        arrived(core_a.at[b, :, pl.ds(half_q, half_o)], core_s.at[1, j], core_r.at[1, j])
-        core_a[b, :, 0:half_q] = (
-            core_a[b, :, 0:half_q].astype(f32) + gq[b, :, cols(c, half_q)].astype(f32)
-        ).astype(bf16)
-        core_a[b, :, half_q:wide] = (
-            core_a[b, :, half_q:wide].astype(f32) + go[b, :, cols(c, half_o)].astype(f32)
-        ).astype(bf16)
+        arrived(core_a.at[b], core_s.at[0, j], core_r.at[0, j])
+        first, second = grad_a(b, c)
+        core_a[b, :, 0:half_q] = (core_a[b, :, 0:half_q].astype(f32) + first).astype(bf16)
+        core_a[b, :, half_q:wide] = (core_a[b, :, half_q:wide].astype(f32) + second).astype(bf16)
 
     def ready_b(j):
         b = me.at(order_b[j])
+        first, second = grad_b(b, c * 2 + x)
+        first = first + core_b[b, x, :, 0:quarter].astype(f32)
+        second = second + core_b[b, x, :, quarter : 2 * quarter].astype(f32)
         arrived(chip_b.at[b], chip_s.at[j], chip_r.at[j])
-        chip_b[b, :, 0:quarter] = (
-            chip_b[b, :, 0:quarter].astype(f32)
-            + (
-                gi[b, :, cols(c * 2 + x, quarter)].astype(f32)
-                + core_i[b, :, cols(x, quarter)].astype(f32)
-            )
-        ).astype(bf16)
+        chip_b[b, :, 0:quarter] = (chip_b[b, :, 0:quarter].astype(f32) + first).astype(bf16)
         chip_b[b, :, quarter : 2 * quarter] = (
-            chip_b[b, :, quarter : 2 * quarter].astype(f32)
-            + (gb[b, c * 2 + x].astype(f32) + core_b[b, x].astype(f32))
+            chip_b[b, :, quarter : 2 * quarter].astype(f32) + second
         ).astype(bf16)
 
     def step(unit, way, t):
@@ -420,31 +441,33 @@
         copy.wait_send()
 
 
-def reduce_gradients(n, d_qkv, d_out, d_in, d_back, small):
-    rows = d_qkv.shape[0] // n
-    bf16, f32 = jnp.bfloat16, jnp.float32
-    operands = (
-        d_qkv.reshape(n, rows, -1),
-        d_out.reshape(n, rows, -1),
-        d_in.reshape(n, rows, -1),
-        d_back.reshape(n, 4, rows, -1),
-        small,
-    )
-    quarter = d_in.shape[1] // 4
-    wide = (d_qkv.shape[1] + d_out.shape[1]) // 2
+def reduce_gradients(n, pairs, small):
+    f32, bf16 = jnp.float32, jnp.bfloat16
+    tokens = pairs[0][0].shape[0]
+    turned = [left.T for left, _ in pairs]
+    rows = turned[0].shape[0] // n
+    turned = [a.reshape(n, rows, tokens) for a in turned[:3]] + [
+        turned[3].reshape(n, 4, rows, tokens)
+    ]
+    grads = [right for _, right in pairs]
+    operands = (*turned, *grads, small)
+    quarter = grads[2].shape[1] // 4
+    wide = (grads[0].shape[1] + grads[1].shape[1]) // 2
+    shapes = [(rows, g.shape[1]) for g in grads[:3]] + [(4, rows, grads[3].shape[1]), small.shape[1:]]
     most = n // 2
     dma = pltpu.SemaphoreType.DMA
     vmem = pltpu.VMEM
     block = (rows, wide)
     outs = pl.pallas_call(
         functools.partial(reduce_kernel, n),
-        out_shape=[jax.ShapeDtypeStruct(a.shape[1:], f32) for a in operands],
-        in_specs=[pl.BlockSpec(memory_space=pltpu.VMEM)] * 5,
+        out_shape=[jax.ShapeDtypeStruct(shape, f32) for shape in shapes],
+        in_specs=[pl.BlockSpec(memory_space=pltpu.VMEM)] * 9,
         out_specs=[pl.BlockSpec(memory_space=pltpu.VMEM)] * 5,
         scratch_shapes=[
             vmem((n,) + block, bf16),
-            vmem((n, rows, 2 * quarter), bf16),
-            vmem((n, 2, rows, quarter), bf16),
+            vmem((n, 2, rows, 2 * quarter), bf16),
+            vmem((n,) + block, bf16),
+            vmem((n, 2, rows, 2 * quarter), bf16),
             vmem((n, rows, 2 * quarter), bf16),
             vmem((n, rows, 2 * quarter), bf16),
             vmem((2, most) + block, bf16),
@@ -456,8 +479,8 @@
             vmem(small.shape, f32),
             vmem(small.shape, f32),
             vmem(small.shape, f32),
-            dma((4, n)),
-            dma((4, n)),
+            dma((2, n)),
+            dma((2, n)),
             dma((n,)),
             dma((n,)),
             dma((2, 2, most)),
@@ -607,14 +630,12 @@
     d_shift_two = jnp.sum(grad_final, 0)
     grad_mid = norm_back(grad_final * full_gain_two.astype(jnp.float32), unit_two, scale_two)
     grad_branch = grad_mid.astype(jnp.bfloat16)
-    d_w_back = jnp.einsum("tf,td->fd", activated, grad_branch, preferred_element_type=jnp.float32)
     d_bias_back = jnp.sum(grad_branch.astype(jnp.float32), 0)
     grad_act = jnp.einsum(
         "td,fd->tf", grad_branch, full_back, preferred_element_type=jnp.float32
     )
     unused_value, gelu_pull = jax.vjp(gelu_exact, inner_sum)
     grad_inner = gelu_pull(grad_act)[0].astype(jnp.bfloat16)
-    d_w_in = jnp.einsum("td,tf->df", first_low, grad_inner, preferred_element_type=jnp.float32)
     d_bias_in = jnp.sum(grad_inner.astype(jnp.float32), 0)
     grad_first = (
         jnp.einsum("tf,df->td", grad_inner, full_in, preferred_element_type=jnp.float32) + grad_mid
@@ -623,7 +644,6 @@
     d_shift_one = jnp.sum(grad_first, 0)
     grad_res = norm_back(grad_first * full_gain_one.astype(jnp.float32), unit_one, scale_one)
     grad_attn = grad_res.astype(jnp.bfloat16)
-    d_w_out = jnp.einsum("td,te->de", mixed_heads, grad_attn, preferred_element_type=jnp.float32)
     d_bias_out = jnp.sum(grad_attn.astype(jnp.float32), 0)
     grad_mixed = jnp.einsum(
         "te,de->td", grad_attn, full_out, preferred_element_type=jnp.float32
@@ -649,14 +669,18 @@
     grad_keys = grad_keys.reshape(row_count, model_width)
     grad_values = grad_values.reshape(row_count, model_width)
     grad_qkv = jnp.concatenate([grad_query, grad_keys, grad_values], 1)
-    d_w_qkv = jnp.einsum("td,te->de", tokens, grad_qkv, preferred_element_type=jnp.float32)
     d_bias_qv = jnp.concatenate(
         [jnp.sum(grad_query.astype(jnp.float32), 0), jnp.sum(grad_values.astype(jnp.float32), 0)], 0
     )
     grad_tokens = (
         jnp.einsum("te,de->td", grad_qkv, full_qkv, preferred_element_type=jnp.float32) + grad_res
     )
-    low_grads = [g.astype(jnp.bfloat16) for g in (d_w_qkv, d_w_out, d_w_in, d_w_back)]
+    pairs = (
+        (tokens, grad_qkv),
+        (mixed_heads, grad_attn),
+        (first_low, grad_inner),
+        (activated, grad_branch),
+    )
     small_grads = pack_small(
         (
             d_bias_qv,
@@ -670,7 +694,7 @@
         ),
         n_shard,
     )
-    summed = reduce_gradients(n_shard, *low_grads, small_grads)
+    summed = reduce_gradients(n_shard, pairs, small_grads)
     if n_rep > QUAD:
         summed = [lax.psum(g, "rep") * (1.0 / QUAD) for g in summed]
     d_qkv, d_out, d_in, d_back, packed = summed

time: 254 us -> 235 us (0.925)
  local copies, waits for them, and re-layouts: 21.8 us -> 14.3 us
  other arithmetic: 8.94 us -> 3.53 us
  matrix products: 42.9 us -> 39.5 us
  Pallas kernels: 179 us -> 176 us
    dot_general x4 -> x0, matrix products: 12.7 us -> none  [the longest x1 3.64 us: body(): jnp.einsum('td,tf->df', first_low, grad_inner, preferred_element_type=jnp...]
    dot_general x1, matrix products: 0.91 us -> 7.14 us  [body(): jnp.dot(activated, full_back, preferred_element_type=jnp.float32)]
    reshape x9, local copies, waits for them, and re-layouts: 7.28 us -> 1.81 us  [pack_small(): joined = jnp.concatenate([v.reshape(n, -1) for v in parts], 1)]
    pallas_call x1, Pallas kernels: 116 us -> 113 us  [reduce_gradients(): pl.pallas_call(functools.partial(reduce_kernel, n), out_shape=[jax.ShapeD...]
    unnamed x99 -> x39, local copies, waits for them, and re-layouts: 6.98 us -> 5.86 us
where the time goes in v2:
time: 235 us; the launch traced here: 234 us
  Pallas kernels  176 us (75%)
  matrix products  39.5 us (17%)
  local copies, waits for them, and re-layouts  14.3 us (6%)
  other arithmetic  3.53 us (2%)
    pallas_call x1, Pallas kernels, reduce_gradients(): pl.pallas_call(functools.partial(reduce_kernel, n), out_shape=[jax.ShapeD...  113 us
    pallas_call x1, Pallas kernels, gather_weights(): pl.pallas_call(functools.partial(gather_kernel, n), out_shape=[jax.ShapeD...  62.7 us
    dot_general x1, matrix products, body(): jnp.dot(first_low, full_in, preferred_element_type=jnp.float32)  7.87 us
    dot_general x1, matrix products, body(): jnp.einsum('td,fd->tf', grad_branch, full_back, preferred_element_type=jn...  7.35 us
    dot_general x1, matrix products, body(): jnp.dot(activated, full_back, preferred_element_type=jnp.float32)  7.14 us
    unnamed x39, local copies, waits for them, and re-layouts  5.86 us

profile of v2, /device:TPU:0, one launch (start us, length us, event | category | flops | bytes accessed | tf_op | source)
XLA Modules:
  0.0 234.2 jit_solution(14181130112133038710)
XLA Ops:
  0.7 0.7 reshape.300
  1.4 0.7 reshape.298
  2.0 0.8 concatenate.17
  2.9 0.6 pad_reduce_fusion
  3.5 62.7 %gather_weights.1 = (bf16[8,96,2304]{2,1,0:T(8,128)(2,1)}, bf16[8,96,768]{2,1,0:T(8,128)(2,1)}, bf16[8,96,3072]{2,1,0:T(8,128)(2,1)}, bf16[8,4,96,768]{3,2,1,0:T(8,128)(2,1)}, bf16[8,16,128]{2,1,0:T(8,128)(2,1)}) custom-call(bf16[96,2304]{1,0:T(8,128)(2,1)} %refs_0_.1, bf16[96,768]{1,0:T(8,128)(2,1)} %refs_1_.1, bf16[96,3072]{1,0:T(8,128)(2,1)} %refs_2_.1, ...), custom_call_target="tpu_custom_call" | custom-call | tf_op jit(solution)/shard_map/gather_weights/pallas_call | solution.py:201
  66.2 0.8 copy.61
  67.2 3.1 %convolution_bitcast_fusion = f32[128,2304]{0,1:T(8,128)S(1)} fusion(bf16[768,2304]{1,0:T(8,128)(2,1)} %bitcast.161, bf16[128,768]{1,0:T(8,128)(2,1)S(1)} %copy-done.3), kind=kOutput, calls=%fused_computation.1 | convolution fusion | flops 452984832 | bytes 4915200 | tf_op jit(solution)/shard_map/dot_general | solution.py:589
  71.1 1.3 fusion.50
  74.5 7.9 %fusion.4 = (bf16[3072,128]{0,1:T(8,128)(2,1)}, f32[128,3072]{1,0:T(8,128)}) fusion(f32[3072]{0:T(1024)S(1)} %reshape.342, bf16[768,3072]{1,0:T(8,128)(2,1)} %bitcast.165, f32[128,768]{1,0:T(8,128)S(1)} %get-tuple-element.70, f32[768]{0:T(1024)S(1)} %reshape.341, f32[768]{0:T(1024)S(1)} %reshape.340, f32[128]{0:T(128)S(1)} %add_rsqrt_fusion.1, ...), kind=kOutput, calls=%fused_computation.8 | convolution fusion | flops 630423552 | bytes 7490560 | tf_op jit(solution)/shard_map/dot_general | solution.py:618
  82.5 7.1 %fusion.52 = (f32[128]{0:T(128)S(1)}, f32[128,768]{1,0:T(8,128)S(1)}) fusion(f32[768]{0:T(1024)S(1)} %reshape.343, bf16[3072,768]{1,0:T(8,128)(2,1)} %bitcast.197, f32[128,3072]{1,0:T(8,128)} %get-tuple-element.76, f32[768]{0:T(1024)S(1)} %reshape.341, f32[768]{0:T(1024)S(1)} %reshape.340, f32[128]{0:T(128)S(1)} %add_rsqrt_fusion.1, ...), kind=kOutput, calls=%fused_computation.133 | convolution fusion | flops 630226816 | bytes 7088640 | tf_op jit(solution)/shard_map/dot_general | solution.py:622
  90.3 0.9 convert_reduce_fusion.1
  91.2 7.4 %convert_reduce_fusion = (f32[3072]{0:T(1024)S(1)}, bf16[128,3072]{1,0:T(8,128)(2,1)S(1)}) fusion(f32[128,3072]{1,0:T(8,128)} %get-tuple-element.76, bf16[128,768]{1,0:T(8,128)(2,1)S(1)} %get-tuple-element.43.refs_7_, bf16[3072,768]{1,0:T(8,128)(2,1)} %bitcast.198), kind=kOutput, calls=%fused_computation.14 | convolution fusion | flops 633074688 | bytes 7286784 | tf_op jit(solution)/shard_map/td,fd->tf/dot_general | solution.py:634
  98.6 4.0 %convolution_add_fusion.3 = f32[128,768]{1,0:T(8,128)S(1)} fusion(bf16[128,3072]{1,0:T(8,128)(2,1)S(1)} %get-tuple-element.45.refs_6_, bf16[768,3072]{1,0:T(8,128)(2,1)} %bitcast.166, f32[128]{0:T(128)S(1)} %get-tuple-element.81, f32[128,768]{1,0:T(8,128)S(1)} %get-tuple-element.72, f32[128]{0:T(128)S(1)} %broadcast_multiply_fusion.4, ...), kind=kOutput, calls=%fused_computation.52 | convolution fusion | flops 604962816 | bytes 6493696 | tf_op jit(solution)/shard_map/tf,df->td/dot_general | solution.py:641
  102.9 0.9 convert_reduce_fusion.2
  104.6 1.5 multiply_reduce_fusion
  106.7 0.7 convert_reduce_fusion.3
  109.6 1.5 copy.51
  111.4 113.2 %reduce_gradients.1 = (f32[96,2304]{1,0:T(8,128)}, f32[96,768]{1,0:T(8,128)S(1)}, f32[96,3072]{1,0:T(8,128)}, f32[4,96,768]{2,1,0:T(8,128)}, f32[16,128]{1,0:T(8,128)S(1)}) custom-call(bf16[8,96,128]{2,1,0:T(8,128)(2,1)S(1)} %bitcast.156, bf16[8,96,128]{2,1,0:T(8,128)(2,1)S(1)} %bitcast.154, bf16[8,96,128]{2,1,0:T(8,128)(2,1)S(1)} %bitcast.155, ...), custom_call_target="tpu_custom_call" | custom-call | tf_op jit(solution)/shard_map/reduce_gradients/pallas_call | solution.py:461
  225.1 0.7 slice_reduce_fusion
  226.4 4.1 %convolution_add_fusion.2 = f32[128,768]{1,0:T(8,128)} fusion(f32[128,768]{1,0:T(8,128)S(1)} %copy-done.10, bf16[768,2304]{1,0:T(8,128)(2,1)} %bitcast.162, bf16[128,768]{1,0:T(8,128)(2,1)S(1)} %copy-done.9, bf16[128,768]{1,0:T(8,128)(2,1)S(1)} %copy-done.7, bf16[128,768]{1,0:T(8,128)(2,1)S(1)} %copy-done.5), kind=kOutput, calls=%fused_computation.49 | convolution fusion | flops 454852608 | bytes 4915200 | tf_op jit(solution)/shard_map/te,de->td/dot_general | solution.py:676
  230.5 0.9 copy.66
  231.4 0.7 copy.67
  232.1 1.0 copy.68
  233.2 1.0 copy.69
  (88 shorter events, 8.8 us)
Async XLA Ops:
  0.6 66.6 %copy-start.3 = (bf16[128,768]{1,0:T(8,128)(2,1)S(1)}, bf16[128,768]{1,0:T(8,128)(2,1)}, u32[]{:S(2)}) copy-start(bf16[128,768]{1,0:T(8,128)(2,1)} %param.15) | copy-start | bytes 589828
  70.3 0.7 copy-start.15
  72.4 1.3 copy-start
  82.5 7.4 %copy-start.2 = (bf16[128,768]{1,0:T(8,128)(2,1)S(1)}, bf16[128,768]{1,0:T(8,128)(2,1)}, u32[]{:S(2)}) copy-start(bf16[128,768]{1,0:T(8,128)(2,1)} %param.29) | copy-start | bytes 589828
  102.6 1.3 copy-start.1
  104.6 1.6 copy-start.14
  108.3 0.8 copy-start.4
  108.8 0.7 copy-start.6
  109.0 0.7 copy-start.8
  111.3 115.1 %copy-start.5 = (bf16[128,768]{1,0:T(8,128)(2,1)S(1)}, bf16[128,768]{1,0:T(8,128)(2,1)}, u32[]{:S(2)}) copy-start(bf16[128,768]{1,0:T(8,128)(2,1)} %copy-done.4) | copy-start | bytes 589828
  111.3 115.0 %copy-start.7 = (bf16[128,768]{1,0:T(8,128)(2,1)S(1)}, bf16[128,768]{1,0:T(8,128)(2,1)}, u32[]{:S(2)}) copy-start(bf16[128,768]{1,0:T(8,128)(2,1)} %copy-done.6) | copy-start | bytes 589828
  111.3 115.0 %copy-start.9 = (bf16[128,768]{1,0:T(8,128)(2,1)S(1)}, bf16[128,768]{1,0:T(8,128)(2,1)}, u32[]{:S(2)}) copy-start(bf16[128,768]{1,0:T(8,128)(2,1)} %copy-done.8) | copy-start | bytes 589828
  111.3 115.0 %copy-start.10 = (f32[128,768]{1,0:T(8,128)S(1)}, f32[128,768]{1,0:T(8,128)}, u32[]{:S(2)}) copy-start(f32[128,768]{1,0:T(8,128)} %get-tuple-element.48) | copy-start | bytes 1179652
  226.4 4.1 %copy-start.13 = (f32[96,2304]{1,0:T(8,128)S(1)}, f32[96,2304]{1,0:T(8,128)}, u32[]{:S(2)}) copy-start(f32[96,2304]{1,0:T(8,128)} %get-tuple-element.99) | copy-start | bytes 2654212
  230.5 1.6 copy-start.12
  231.4 1.7 copy-start.11

commit v3 on v2

--- a/solution.py
+++ b/solution.py
@@ -536,8 +536,59 @@
     )
 
 
-def gelu_exact(inputs):
-    return jax.nn.gelu(inputs, approximate=False)
+def head_probs(q_ref, k_ref, same, head):
+    scores = lax.dot_general(
+        q_ref[:, head], k_ref[:, head], (((1,), (1,)), ((), ())), preferred_element_type=jnp.float32
+    ) * (1.0 / math.sqrt(HEAD_DIM))
+    scores = jnp.where(same, scores, -1000000000.0)
+    exponent = jnp.exp(scores - jnp.max(scores, -1, keepdims=True))
+    return exponent / jnp.sum(exponent, -1, keepdims=True)
+
+
+def attend_kernel(q_ref, k_ref, v_ref, down_ref, across_ref, mixed_ref):
+    same = down_ref[...] == across_ref[...]
+    for h in range(HEADS):
+        head = slice(h * HEAD_DIM, (h + 1) * HEAD_DIM)
+        probs = head_probs(q_ref, k_ref, same, head).astype(jnp.bfloat16)
+        mixed_ref[:, head] = jnp.dot(
+            probs, v_ref[:, head], preferred_element_type=jnp.float32
+        ).astype(jnp.bfloat16)
+
+
+def attend_back_kernel(q_ref, k_ref, v_ref, g_ref, down_ref, across_ref, out_ref):
+    same = down_ref[...] == across_ref[...]
+    scale = 1.0 / math.sqrt(HEAD_DIM)
+    f32, bf16 = jnp.float32, jnp.bfloat16
+    width = q_ref.shape[1]
+    columns = (((0,), (0,)), ((), ()))
+    for h in range(HEADS):
+        start = h * HEAD_DIM
+        head = slice(start, start + HEAD_DIM)
+        probs = head_probs(q_ref, k_ref, same, head)
+        grad = lax.dot_general(
+            g_ref[:, head], v_ref[:, head], (((1,), (1,)), ((), ())), preferred_element_type=f32
+        )
+        row_dot = jnp.sum(probs * grad, -1, keepdims=True)
+        grad = (probs * (grad - row_dot)).astype(bf16)
+        out_ref[:, head] = (
+            jnp.dot(grad, k_ref[:, head], preferred_element_type=f32) * scale
+        ).astype(bf16)
+        out_ref[:, width + start : width + start + HEAD_DIM] = (
+            lax.dot_general(grad, q_ref[:, head], columns, preferred_element_type=f32) * scale
+        ).astype(bf16)
+        out_ref[:, 2 * width + start : 2 * width + start + HEAD_DIM] = lax.dot_general(
+            probs.astype(bf16), g_ref[:, head], columns, preferred_element_type=f32
+        ).astype(bf16)
+
+
+def on_chip(kernel, shape, *operands):
+    return pl.pallas_call(
+        kernel,
+        out_shape=jax.ShapeDtypeStruct(shape, jnp.bfloat16),
+        in_specs=[pl.BlockSpec(memory_space=pltpu.VMEM)] * len(operands),
+        out_specs=pl.BlockSpec(memory_space=pltpu.VMEM),
+        compiler_params=pltpu.CompilerParams(vmem_limit_bytes=24 * 2**20),
+    )(*operands)
 
 
 def body(
@@ -585,29 +636,15 @@
     ) = unpack_small(packed, sizes)
     model_width = full_out.shape[0]
     row_count = tokens.shape[0]
-    score_scale = 1.0 / math.sqrt(HEAD_DIM)
     qkv = jnp.dot(tokens, full_qkv, preferred_element_type=jnp.float32)
     bias_float = full_bias_qv.astype(jnp.float32)
     query_rows = (qkv[:, :model_width] + bias_float[:model_width]).astype(jnp.bfloat16)
     key_rows = qkv[:, model_width : 2 * model_width].astype(jnp.bfloat16)
     value_rows = (qkv[:, 2 * model_width :] + bias_float[model_width:]).astype(jnp.bfloat16)
-    query_heads = query_rows.reshape(row_count, HEADS, HEAD_DIM)
-    key_heads = key_rows.reshape(row_count, HEADS, HEAD_DIM)
-    value_heads = value_rows.reshape(row_count, HEADS, HEAD_DIM)
-    scores = (
-        jnp.einsum("qhd,khd->hqk", query_heads, key_heads, preferred_element_type=jnp.float32)
-        * score_scale
-    )
-    same_doc = labels[:, None] == labels[None, :]
-    scores = jnp.where(same_doc[None], scores, -1000000000.0)
-    highest = jnp.max(scores, -1, keepdims=True)
-    exponent = jnp.exp(scores - highest)
-    attention = exponent / jnp.sum(exponent, -1, keepdims=True)
-    attention_low = attention.astype(jnp.bfloat16)
-    mixed_heads = jnp.einsum(
-        "hqk,khd->qhd", attention_low, value_heads, preferred_element_type=jnp.float32
-    )
-    mixed_heads = mixed_heads.reshape(row_count, model_width).astype(jnp.bfloat16)
+    down, across = labels[:, None], labels[None, :]
+    mixed_heads = on_chip(
+        attend_kernel, query_rows.shape, query_rows, key_rows, value_rows, down, across
+    )
     attn_out = jnp.dot(
         mixed_heads, full_out, preferred_element_type=jnp.float32
     ) + full_bias_out.astype(jnp.float32)
@@ -618,7 +655,11 @@
     inner_sum = jnp.dot(
         first_low, full_in, preferred_element_type=jnp.float32
     ) + full_bias_in.astype(jnp.float32)
-    activated = gelu_exact(inner_sum).astype(jnp.bfloat16)
+    share = 0.5 * (1.0 + lax.erf(inner_sum * math.sqrt(0.5)))
+    slope = share + inner_sum * jnp.exp(-0.5 * inner_sum * inner_sum) / math.sqrt(2.0 * math.pi)
+    activated, slope = lax.optimization_barrier(
+        ((inner_sum * share).astype(jnp.bfloat16), slope)
+    )
     branch = jnp.dot(
         activated, full_back, preferred_element_type=jnp.float32
     ) + full_bias_back.astype(jnp.float32)
@@ -634,8 +675,7 @@
     grad_act = jnp.einsum(
         "td,fd->tf", grad_branch, full_back, preferred_element_type=jnp.float32
     )
-    unused_value, gelu_pull = jax.vjp(gelu_exact, inner_sum)
-    grad_inner = gelu_pull(grad_act)[0].astype(jnp.bfloat16)
+    grad_inner = (grad_act * slope).astype(jnp.bfloat16)
     d_bias_in = jnp.sum(grad_inner.astype(jnp.float32), 0)
     grad_first = (
         jnp.einsum("tf,df->td", grad_inner, full_in, preferred_element_type=jnp.float32) + grad_mid
@@ -648,27 +688,18 @@
     grad_mixed = jnp.einsum(
         "te,de->td", grad_attn, full_out, preferred_element_type=jnp.float32
     ).astype(jnp.bfloat16)
-    grad_mixed_heads = grad_mixed.reshape(row_count, HEADS, HEAD_DIM)
-    grad_attention = jnp.einsum(
-        "qhd,khd->hqk", grad_mixed_heads, value_heads, preferred_element_type=jnp.float32
-    )
-    row_dot = jnp.sum(attention * grad_attention, -1, keepdims=True)
-    grad_scores = (attention * (grad_attention - row_dot)).astype(jnp.bfloat16)
-    grad_query = (
-        jnp.einsum("hqk,khd->qhd", grad_scores, key_heads, preferred_element_type=jnp.float32)
-        * score_scale
-    ).astype(jnp.bfloat16)
-    grad_keys = (
-        jnp.einsum("hqk,qhd->khd", grad_scores, query_heads, preferred_element_type=jnp.float32)
-        * score_scale
-    ).astype(jnp.bfloat16)
-    grad_values = jnp.einsum(
-        "hqk,qhd->khd", attention_low, grad_mixed_heads, preferred_element_type=jnp.float32
-    ).astype(jnp.bfloat16)
-    grad_query = grad_query.reshape(row_count, model_width)
-    grad_keys = grad_keys.reshape(row_count, model_width)
-    grad_values = grad_values.reshape(row_count, model_width)
-    grad_qkv = jnp.concatenate([grad_query, grad_keys, grad_values], 1)
+    grad_qkv = on_chip(
+        attend_back_kernel,
+        (row_count, 3 * model_width),
+        query_rows,
+        key_rows,
+        value_rows,
+        grad_mixed,
+        down,
+        across,
+    )
+    grad_query = grad_qkv[:, :model_width]
+    grad_values = grad_qkv[:, 2 * model_width :]
     d_bias_qv = jnp.concatenate(
         [jnp.sum(grad_query.astype(jnp.float32), 0), jnp.sum(grad_values.astype(jnp.float32), 0)], 0
     )

time: 235 us -> 230 us (0.979)
  matrix products: 39.5 us -> 24.7 us
  Pallas kernels: 176 us -> 186 us
    pallas_call x0 -> x2, Pallas kernels: none -> 10.4 us  [on_chip(): pl.pallas_call(kernel, out_shape=jax.ShapeDtypeStruct(shape, jnp.bfloat16...]
    dot_general x1, matrix products: 7.14 us -> 3.46 us  [body(): jnp.dot(activated, full_back, preferred_element_type=jnp.float32)]
    dot_general x5 -> x0, matrix products: 3.56 us -> none  [the longest x1 1.53 us: body(): jnp.einsum('qhd,khd->hqk', grad_mixed_heads, value_heads, preferred_eleme...]
    dot_general x1, matrix products: 7.87 us -> 4.99 us  [body(): jnp.dot(first_low, full_in, preferred_element_type=jnp.float32)]
    dot_general x1, matrix products: 7.35 us -> 4.51 us  [body(): jnp.einsum('td,fd->tf', grad_branch, full_back, preferred_element_type=jn...]
    transpose x2 -> x4, local copies, waits for them, and re-layouts: 0.32 us -> 2.95 us  [reduce_gradients(): turned = [left.T for left, _ in pairs]]
    unnamed x39 -> x27, local copies, waits for them, and re-layouts: 5.86 us -> 5.06 us
where the time goes in v3:
time: 230 us; the launch traced here: 229 us
  Pallas kernels  186 us (81%)
  matrix products  24.7 us (11%)
  local copies, waits for them, and re-layouts  14.1 us (6%)
  other arithmetic  3.14 us (1%)
    pallas_call x1, Pallas kernels, reduce_gradients(): pl.pallas_call(functools.partial(reduce_kernel, n), out_shape=[jax.ShapeD...  113 us
    pallas_call x1, Pallas kernels, gather_weights(): pl.pallas_call(functools.partial(gather_kernel, n), out_shape=[jax.ShapeD...  62.7 us
    pallas_call x2, Pallas kernels, on_chip(): pl.pallas_call(kernel, out_shape=jax.ShapeDtypeStruct(shape, jnp.bfloat16...  10.4 us
    unnamed x27, local copies, waits for them, and re-layouts  5.06 us
    dot_general x1, matrix products, body(): jnp.dot(first_low, full_in, preferred_element_type=jnp.float32)  4.99 us

profile of v3, /device:TPU:0, one launch (start us, length us, event | category | flops | bytes accessed | tf_op | source)
XLA Modules:
  0.0 229.1 jit_solution(17923914361823040887)
XLA Ops:
  0.7 0.7 reshape.242
  1.4 0.7 reshape.240
  2.0 0.8 concatenate.14
  2.9 0.6 pad_reduce_fusion
  3.5 62.7 %gather_weights.1 = (bf16[8,96,2304]{2,1,0:T(8,128)(2,1)}, bf16[8,96,768]{2,1,0:T(8,128)(2,1)}, bf16[8,96,3072]{2,1,0:T(8,128)(2,1)}, bf16[8,4,96,768]{3,2,1,0:T(8,128)(2,1)}, bf16[8,16,128]{2,1,0:T(8,128)(2,1)}) custom-call(bf16[96,2304]{1,0:T(8,128)(2,1)} %refs_0_.1, bf16[96,768]{1,0:T(8,128)(2,1)} %refs_1_.1, bf16[96,3072]{1,0:T(8,128)(2,1)} %refs_2_.1, ...), custom_call_target="tpu_custom_call" | custom-call | tf_op jit(solution)/shard_map/gather_weights/pallas_call | solution.py:201
  66.2 0.8 copy.49
  67.2 2.6 %convolution_bitcast_fusion = f32[128,2304]{1,0:T(8,128)S(1)} fusion(bf16[128,768]{1,0:T(8,128)(2,1)S(1)} %copy-done.5, bf16[768,2304]{1,0:T(8,128)(2,1)} %bitcast.78), kind=kOutput, calls=%fused_computation | convolution fusion | flops 452984832 | bytes 4915200 | tf_op jit(solution)/shard_map/dot_general | solution.py:639
  70.6 4.3 %shard_map.254 = bf16[128,768]{1,0:T(8,128)(2,1)S(1)} custom-call(bf16[128,768]{1,0:T(8,128)(2,1)S(1)} %get-tuple-element.56.q_ref, bf16[128,768]{1,0:T(8,128)(2,1)S(1)} %slice.148.k_ref, bf16[128,768]{1,0:T(8,128)(2,1)S(1)} %get-tuple-element.55.v_ref, s32[128,1]{1,0:T(8,128)S(1)} %copy.37.down_ref, s32[1,128]{1,0:T(1,128)S(1)} %bitcast.71), custom_call_target="tpu_custom_call" | custom-call | tf_op jit(solution)/shard_map/pallas_call | solution.py:585
  75.9 5.0 %fusion.4 = (f32[128,3072]{1,0:T(8,128)}, bf16[128,3072]{1,0:T(8,128)(2,1)S(1)}) fusion(f32[3072]{0:T(1024)S(1)} %reshape.277, bf16[768,3072]{1,0:T(8,128)(2,1)} %bitcast.82, f32[128,768]{1,0:T(8,128)S(1)} %get-tuple-element.74, f32[768]{0:T(1024)S(1)} %reshape.276, f32[768]{0:T(1024)S(1)} %reshape.275, f32[128]{0:T(128)S(1)} %add_rsqrt_fusion.1, ...), kind=kOutput, calls=%fused_computation.8 | convolution fusion | flops 608796672 | bytes 7490560 | tf_op jit(solution)/shard_map/dot_general | solution.py:655
  81.0 3.5 %fusion.19 = (f32[128]{0:T(128)S(1)}, f32[128,768]{1,0:T(8,128)S(1)}) fusion(f32[768]{0:T(1024)S(1)} %reshape.278, bf16[128,3072]{1,0:T(8,128)(2,1)S(1)} %get-tuple-element.30, bf16[3072,768]{1,0:T(8,128)(2,1)} %bitcast.76, f32[768]{0:T(1024)S(1)} %reshape.276, f32[768]{0:T(1024)S(1)} %reshape.275, f32[128]{0:T(128)S(1)} %add_rsqrt_fusion.1, ...), kind=kOutput, calls=%fused_computation.79 | convolution fusion | flops 604667776 | bytes 6302208 | tf_op jit(solution)/shard_map/dot_general | solution.py:663
  85.1 0.9 convert_reduce_fusion.1
  86.1 4.5 %convert_reduce_fusion = (f32[3072]{0:T(1024)S(1)}, bf16[128,3072]{1,0:T(8,128)(2,1)S(1)}) fusion(f32[128,3072]{1,0:T(8,128)} %get-tuple-element.32, bf16[128,768]{1,0:T(8,128)(2,1)S(1)} %get-tuple-element.49.refs_7_, bf16[3072,768]{1,0:T(8,128)(2,1)} %bitcast.77), kind=kOutput, calls=%fused_computation.9 | convolution fusion | flops 605549568 | bytes 7286784 | tf_op jit(solution)/shard_map/td,fd->tf/dot_general | solution.py:675
  90.6 4.1 %convolution_add_fusion.3 = f32[128,768]{1,0:T(8,128)S(1)} fusion(bf16[128,3072]{1,0:T(8,128)(2,1)S(1)} %get-tuple-element.78.refs_6_, bf16[768,3072]{1,0:T(8,128)(2,1)} %bitcast.83, f32[128]{0:T(128)S(1)} %get-tuple-element.79, f32[128,768]{1,0:T(8,128)S(1)} %get-tuple-element.76, f32[128]{0:T(128)S(1)} %broadcast_multiply_fusion.4, ...), kind=kOutput, calls=%fused_computation.15 | convolution fusion | flops 604962816 | bytes 6493696 | tf_op jit(solution)/shard_map/tf,df->td/dot_general | solution.py:681
  95.0 0.9 convert_reduce_fusion.2
  96.5 6.1 %shard_map.255.refs_4_ = bf16[128,2304]{1,0:T(8,128)(2,1)S(1)} custom-call(bf16[128,768]{1,0:T(8,128)(2,1)S(1)} %get-tuple-element.56.q_ref, bf16[128,768]{1,0:T(8,128)(2,1)S(1)} %slice.148.k_ref, bf16[128,768]{1,0:T(8,128)(2,1)S(1)} %get-tuple-element.55.v_ref, bf16[128,768]{1,0:T(8,128)(2,1)S(1)} %convolution_convert_fusion.g_ref, ...), custom_call_target="tpu_custom_call" | custom-call | tf_op jit(solution)/shard_map/pallas_call | solution.py:585
  103.5 1.5 copy.42
  105.3 1.1 copy.39
  106.4 113.1 %reduce_gradients.1 = (f32[96,2304]{1,0:T(8,128)}, f32[96,768]{1,0:T(8,128)S(1)}, f32[96,3072]{1,0:T(8,128)}, f32[4,96,768]{2,1,0:T(8,128)}, f32[16,128]{1,0:T(8,128)S(1)}) custom-call(bf16[8,96,128]{2,1,0:T(8,128)(2,1)S(1)} %bitcast.68, bf16[8,96,128]{2,1,0:T(8,128)(2,1)S(1)} %bitcast.67, bf16[8,96,128]{2,1,0:T(8,128)(2,1)S(1)} %bitcast.66, ...), custom_call_target="tpu_custom_call" | custom-call | tf_op jit(solution)/shard_map/reduce_gradients/pallas_call | solution.py:461
  220.1 0.7 slice_reduce_fusion
  221.3 4.1 %convolution_add_fusion.2 = f32[128,768]{1,0:T(8,128)} fusion(f32[128,768]{1,0:T(8,128)S(1)} %copy-done.6, bf16[128,2304]{1,0:T(8,128)(2,1)S(1)} %shard_map.255.refs_4_, bf16[768,2304]{1,0:T(8,128)(2,1)} %bitcast.79), kind=kOutput, calls=%fused_computation.14 | convolution fusion | flops 453083136 | bytes 4915200 | tf_op jit(solution)/shard_map/te,de->td/dot_general | solution.py:707
  225.5 0.9 copy.54
  226.4 0.7 copy.55
  227.1 1.0 copy.56
  228.1 1.0 copy.57
  (68 shorter events, 5.8 us)
Async XLA Ops:
  0.6 66.6 %copy-start.5 = (bf16[128,768]{1,0:T(8,128)(2,1)S(1)}, bf16[128,768]{1,0:T(8,128)(2,1)}, u32[]{:S(2)}) copy-start(bf16[128,768]{1,0:T(8,128)(2,1)} %param.15) | copy-start | bytes 589828
  69.9 0.7 copy-start
  69.9 5.2 %copy-start.1 = (bf16[8,96,768]{2,1,0:T(8,128)(2,1)S(1)}, bf16[8,96,768]{2,1,0:T(8,128)(2,1)}, u32[]{:S(2)}) copy-start(bf16[8,96,768]{2,1,0:T(8,128)(2,1)} %get-tuple-element.28) | copy-start | bytes 3538948
  80.9 3.5 %copy-start.3 = (bf16[128,3072]{1,0:T(8,128)(2,1)}, bf16[128,3072]{1,0:T(8,128)(2,1)S(1)}, u32[]{:S(2)}) copy-start(bf16[128,3072]{1,0:T(8,128)(2,1)S(1)} %get-tuple-element.30) | copy-start | bytes 2359300
  81.0 3.8 %copy-start.4 = (bf16[128,768]{1,0:T(8,128)(2,1)S(1)}, bf16[128,768]{1,0:T(8,128)(2,1)}, u32[]{:S(2)}) copy-start(bf16[128,768]{1,0:T(8,128)(2,1)} %param.29) | copy-start | bytes 589828
  94.7 1.3 copy-start.2
  106.3 115.0 %copy-start.6 = (f32[128,768]{1,0:T(8,128)S(1)}, f32[128,768]{1,0:T(8,128)}, u32[]{:S(2)}) copy-start(f32[128,768]{1,0:T(8,128)} %get-tuple-element.52) | copy-start | bytes 1179652
  221.3 4.1 %copy-start.9 = (f32[96,2304]{1,0:T(8,128)S(1)}, f32[96,2304]{1,0:T(8,128)}, u32[]{:S(2)}) copy-start(f32[96,2304]{1,0:T(8,128)} %get-tuple-element.97) | copy-start | bytes 2654212
  225.5 1.6 copy-start.8
  226.4 1.7 copy-start.7
